TPU v7x, 256 devices: a whole 4x4x8 slice. The times are simulated.
256 devices in a mesh: rcv: 16 (over y, x), src: 8 (over z), freq: 2 (over core).
Axes of the slice: x: 4, y: 4, z: 8, core: 2. Of those that a mesh axis runs over, the one named last changes fastest.
Arguments:
- slice_data: bfloat16 [4, 6144, 6144], P('freq', 'rcv', 'src'), parts along dimension 0, may hold values from -6 to 6
Outputs:
- multiples: float32 [4, 6144, 6144], P('freq', 'rcv', 'src'), parts along dimension 0
There are 2 independent parts, one for each index of `freq`. A program takes and returns all parts, laid end to end along the dimension named above; each array names one. Nothing has to cross between parts.
All inputs are finite; a program needn't handle non-finite values.
Results may differ from a plain program's by a relative error of at most 0.0003.
Values may be sent and summed in bfloat16 or wider, within the bound.
No kernel may reach another device: no remote copies, remote signals or barrier semaphores. Data moves between devices by JAX's collectives and lax.ppermute only.
A program may use at most 128 MiB of HBM per device.

v0:
```python
import jax
import jax.numpy as jnp
from jax import lax
from jax.sharding import PartitionSpec as P

NS = 6144


def per_device(slice_data):
    panel = lax.all_gather(slice_data, "src", axis=2, tiled=True)
    piece = lax.all_gather(slice_data, "rcv", axis=1, tiled=True)
    left_re = panel[0]
    left_im = panel[1]
    right_re = piece[0]
    right_im = piece[1]
    real_part = jnp.dot(left_re, right_re, preferred_element_type=jnp.float32) - jnp.dot(
        left_im, right_im, preferred_element_type=jnp.float32
    )
    imag_part = jnp.dot(left_re, right_im, preferred_element_type=jnp.float32) + jnp.dot(
        left_im, right_re, preferred_element_type=jnp.float32
    )
    scale = 1.0 / jnp.sqrt(jnp.float32(NS))
    return jnp.stack([real_part * scale, imag_part * scale])


def solution(mesh):
    in_specs = (P("freq", "rcv", "src"),)
    out_specs = P("freq", "rcv", "src")
    return jax.shard_map(
        per_device, mesh=mesh, in_specs=in_specs, out_specs=out_specs, check_vma=False
    )
```

profile of v0, /device:TPU:96, one launch (start us, length us, event | category | flops | bytes accessed | tf_op | source)
XLA Modules:
  0.0 280.5 jit_solution(8319953703873839633)
XLA Ops:
  6.5 0.0 all-gather.3.cloned.1.call-start
  6.5 0.7 all-gather.3.cloned.1.call-update
  7.3 0.0 all-gather.5.cloned.1.call-start
  7.3 0.7 all-gather.5.cloned.1.call-update
  8.0 106.5 %all-gather.3.cloned.1.call-done = bf16[2,384,6144]{2,1,0:T(8,128)(2,1)} async-done(((bf16[2,384,768]{2,1,0:T(8,128)(2,1)}), bf16[2,384,6144]{2,1,0:T(8,128)(2,1)}) %all-gather.3.cloned.1.call-update) | async-done | bytes 9437200 | tf_op jit(solution)/shard_map/all_gather | solution.py:10
  114.5 128.7 %all-gather.5.cloned.1.call-done = bf16[2,6144,768]{2,1,0:T(8,128)(2,1)} async-done(((bf16[2,384,768]{2,1,0:T(8,128)(2,1)}), bf16[2,6144,768]{2,1,0:T(8,128)(2,1)}) %all-gather.5.cloned.1.call-update) | async-done | bytes 18874384 | tf_op jit(solution)/shard_map/all_gather | solution.py:11
  243.1 0.0 copy-start
  243.1 8.6 %fusion = f32[384,768]{1,0:T(8,128)S(1)} fusion(bf16[2,6144,768]{2,1,0:T(8,128)(2,1)} %all-gather.5.cloned.1.call-done, bf16[2,384,6144]{2,1,0:T(8,128)(2,1)} %all-gather.3.cloned.1.call-done), kind=kOutput, calls=%fused_computation.2 | convolution fusion | flops 3623878656 | bytes 15335424 | tf_op jit(solution)/shard_map/dot_general | solution.py:19
  251.8 1.9 copy-done
  253.7 6.1 %fusion.1 = f32[384,768]{1,0:T(8,128)S(1)} fusion(bf16[2,6144,768]{2,1,0:T(8,128)(2,1)S(1)} %copy-done, bf16[2,384,6144]{2,1,0:T(8,128)(2,1)} %all-gather.3.cloned.1.call-done), kind=kOutput, calls=%fused_computation.3 | convolution fusion | flops 3623878656 | bytes 15335424 | tf_op jit(solution)/shard_map/dot_general | solution.py:16
  259.8 6.1 %fusion.7 = f32[1,384,768]{2,1,0:T(8,128)S(1)} fusion(f32[384,768]{1,0:T(8,128)S(1)} %fusion, bf16[2,6144,768]{2,1,0:T(8,128)(2,1)S(1)} %copy-done, bf16[2,384,6144]{2,1,0:T(8,128)(2,1)} %all-gather.3.cloned.1.call-done), kind=kOutput, calls=%fused_computation.12 | convolution fusion | flops 3624468480 | bytes 16515072 | tf_op jit(solution)/shard_map/dot_general | solution.py:19
  266.0 6.1 %fusion.9 = f32[1,384,768]{2,1,0:T(8,128)S(1)} fusion(f32[384,768]{1,0:T(8,128)S(1)} %fusion.1, bf16[2,6144,768]{2,1,0:T(8,128)(2,1)S(1)} %copy-done, bf16[2,384,6144]{2,1,0:T(8,128)(2,1)} %all-gather.3.cloned.1.call-done), kind=kOutput, calls=%fused_computation.14 | convolution fusion | flops 3624468480 | bytes 16515072 | tf_op jit(solution)/shard_map/dot_general | solution.py:16
  272.1 1.6 pad_maximum_fusion
Async XLA Ops:
  6.5 107.9 %all-gather.3.cloned.1.call-start = ((), (), s32[]{:S(2)}) async-start(), calls=%async_computation | async-start | bytes 10616832 | tf_op jit(solution)/shard_map/all_gather | solution.py:10
  7.3 235.9 %all-gather.5.cloned.1.call-start = ((), (), s32[]{:S(2)}) async-start(), calls=%async_computation.1 | async-start | bytes 20054016 | tf_op jit(solution)/shard_map/all_gather | solution.py:11
  243.1 10.5 %copy-start = (bf16[2,6144,768]{2,1,0:T(8,128)(2,1)S(1)}, bf16[2,6144,768]{2,1,0:T(8,128)(2,1)}, u32[]{:S(2)}) copy-start(bf16[2,6144,768]{2,1,0:T(8,128)(2,1)} %all-gather.5.cloned.1.call-done) | copy-start | bytes 56623108
Sparse Core Ops, SparseCore 0:
  9.1 105.2 all-gather.2
  116.9 126.1 all-gather.4
where the time goes:
time: 283 us; the launch traced here: 281 us
  waiting for transfers between devices  237 us (84%)
  matrix products  27.1 us (10%)
  between operations  13.4 us (5%)
    all_gather x1, waiting for transfers between devices, per_device(): piece = lax.all_gather(slice_data, 'rcv', axis=1, tiled=True)  129 us
    all_gather x1, waiting for transfers between devices, per_device(): panel = lax.all_gather(slice_data, 'src', axis=2, tiled=True)  106 us
    dot_general x1, matrix products, per_device(): jnp.dot(left_im, right_re, preferred_element_type=jnp.float32)  8.65 us
    dot_general x1, matrix products, per_device(): jnp.dot(left_im, right_im, preferred_element_type=jnp.float32)  6.14 us
    dot_general x1, matrix products, per_device(): jnp.dot(left_re, right_im, preferred_element_type=jnp.float32)  6.14 us
    dot_general x1, matrix products, per_device(): jnp.dot(left_re, right_re, preferred_element_type=jnp.float32)  6.13 us
  transfers between devices with their start and end apart: 2, of which 2 were waited for; matrix products, arithmetic and copies ran while one was open for 0% of the time, Pallas kernels for 0%

commit v1 on v0

v1 whole, which is shorter than its diff:
```python
import functools

import jax
import jax.numpy as jnp
from jax import lax
from jax.experimental import pallas as pl
from jax.experimental.pallas import tpu as pltpu
from jax.sharding import PartitionSpec as P

NS = 6144
WINDOW = 5


def plane_pairs(first, hop):
    pairs = []
    for y in range(4):
        for x in range(4):
            for core in range(2):
                if (core == 0) == first:
                    target = y * 4 + (x + hop) % 4
                else:
                    target = ((y + hop) % 4) * 4 + x
                pairs.append(((y * 4 + x) * 2 + core, target * 2 + core))
    return pairs


def ring_pairs(hop):
    return [(z * 2 + core, (z + (hop if core == 0 else -hop)) % 8 * 2 + core) for z in range(8) for core in range(2)]


STEPS = (
    ((-1, 0), (0, 0), "a", 1),
    ((1, 0), (0, 0), "a", -1),
    (-1, 0, "z", 1),
    ((2, 0), (-1, 0), "a", 1),
    ((0, 1), (0, 0), "b", -1),
    (1, 0, "z", -1),
    ((0, -1), (0, 0), "b", 1),
    ((-1, 1), (-1, 0), "b", -1),
    (-2, -1, "z", 1),
    ((-1, -1), (-1, 0), "b", 1),
    ((1, 1), (1, 0), "b", -1),
    (2, 1, "z", -1),
    ((1, -1), (1, 0), "b", 1),
    ((0, 2), (0, 1), "b", -1),
    (-3, -2, "z", 1),
    ((2, -1), (2, 0), "b", 1),
    ((2, 1), (2, 0), "b", -1),
    (3, 2, "z", -1),
    ((-1, 2), (-1, -1), "b", 1),
    ((1, 2), (1, 1), "b", -1),
    (4, -3, "z", 1),
    ((2, 2), (2, -1), "b", 1),
)
EARLY = [(0, 0)] + [step[0] for step in STEPS[:18] if step[2] != "z"]
LATE = [step[0] for step in STEPS[18:] if step[2] != "z"]
NEAR = (0, 1, 2, 3, -3, -2, -1)


def move(value, axis, hop):
    if axis == "z":
        return lax.ppermute(value, ("src", "freq"), ring_pairs(hop))
    return lax.ppermute(value, ("rcv", "freq"), plane_pairs(axis == "a", hop))


def place():
    here, row, core = lax.axis_index("src"), lax.axis_index("rcv"), lax.axis_index("freq")
    return here, row // 4, row % 4, core


def owner_of(key):
    _, y, x, core = place()
    a, b = key
    dx, dy = jnp.where(core == 0, a, b), jnp.where(core == 0, b, a)
    return ((y + dy + 4) % 4) * 4 + (x + dx + 4) % 4


def key_code(owner):
    _, y, x, core = place()
    dy, dx = (owner // 4 - y + 4) % 4, (owner % 4 - x + 4) % 4
    return jnp.where(core == 0, dx * 4 + dy, dy * 4 + dx)


def left_code(owner):
    here, _, _, core = place()
    offset = owner // 2 - here + 8
    return jnp.where(core == 0, offset, 16 - offset) % 8


def product(left, right):
    depth, width = right.shape[1:]
    l_re, l_im = left[0], left[1]
    both = jnp.concatenate([jnp.concatenate([l_re, -l_im], axis=1), jnp.concatenate([l_im, l_re], axis=1)], axis=0)
    value = jnp.dot(both, right.reshape(2 * depth, width), preferred_element_type=jnp.float32)
    return value.reshape(2, depth, width)


def pick_left(owner, lefts, keys, target, sem):
    depth = target.shape[-1]
    code = left_code(owner)
    start = pl.multiple_of((owner % 2) * depth, depth)
    for ref, key in zip(lefts, keys):
        @pl.when(code == key % 8)
        def _():
            pltpu.make_async_copy(ref.at[:, :, pl.ds(start, depth)], target, sem).start()


def early_kernel(*refs):
    refs = list(refs)
    lefts = [refs.pop(0) for _ in NEAR]
    rights = [refs.pop(0) for _ in EARLY]
    out, l_buf, r_buf, sems = refs
    owners = [owner_of(key) for key in EARLY]
    ready = [left_code(owner) != 4 for owner in owners]

    def start(k):
        @pl.when(ready[k])
        def _():
            pltpu.make_async_copy(rights[k], r_buf.at[k % 2], sems.at[k % 2, 0]).start()
        pick_left(owners[k], lefts, NEAR, l_buf.at[k % 2], sems.at[k % 2, 1])

    start(0)
    out[...] = jnp.zeros_like(out)
    for k in range(len(EARLY)):
        if k + 1 < len(EARLY):
            start(k + 1)

        @pl.when(ready[k])
        def _():
            pltpu.make_async_copy(rights[k], r_buf.at[k % 2], sems.at[k % 2, 0]).wait()
            pltpu.make_async_copy(lefts[0].at[:, :, pl.ds(0, l_buf.shape[-1])], l_buf.at[k % 2], sems.at[k % 2, 1]).wait()
            out[...] += product(l_buf[k % 2], r_buf[k % 2])


def late_kernel(scale, *refs):
    refs = list(refs)
    keys = NEAR + (4,)
    lefts = [refs.pop(0) for _ in keys]
    rights = [refs.pop(0) for _ in EARLY + LATE]
    total, out, l_buf, r_buf, sems = refs
    here = lax.axis_index("src")
    depth = l_buf.shape[-1]
    tasks = []
    for key in LATE:
        tasks.append((owner_of(key), None))
    for part in range(2):
        owner = 2 * ((here + 4) % 8) + part
        code = key_code(owner)
        tasks.append((owner, code))

    def is_early(code):
        hit = code == 0
        for a, b in EARLY[1:]:
            hit = jnp.logical_or(hit, code == (a % 4) * 4 + b % 4)
        return hit

    for k, (owner, code) in enumerate(tasks):
        if code is None:
            pltpu.make_async_copy(rights[len(EARLY) + k], r_buf.at[k], sems.at[k, 0]).start()
            pick_left(owner, lefts, keys, l_buf.at[k], sems.at[k, 1])
        else:
            for ref, (a, b) in zip(rights, EARLY):
                @pl.when(code == (a % 4) * 4 + b % 4)
                def _():
                    pltpu.make_async_copy(ref, r_buf.at[k], sems.at[k, 0]).start()
            start = pl.multiple_of((owner % 2) * depth, depth)
            pltpu.make_async_copy(lefts[-1].at[:, :, pl.ds(start, depth)], l_buf.at[k], sems.at[k, 1]).start()

    def finish(k, right=True):
        pltpu.make_async_copy(lefts[0].at[:, :, pl.ds(0, depth)], l_buf.at[k], sems.at[k, 1]).wait()

    out[...] = total[...]
    for k, (owner, code) in enumerate(tasks):
        pltpu.make_async_copy(lefts[0].at[:, :, pl.ds(0, depth)], l_buf.at[k], sems.at[k, 1]).wait()

        def work():
            pltpu.make_async_copy(rights[0], r_buf.at[k], sems.at[k, 0]).wait()
            out[...] += product(l_buf[k], r_buf[k])

        if code is None:
            work()
        else:
            pl.when(is_early(code))(work)
    out[...] *= scale


def call(kernel, operands, n_outside, slots, flops, depth, width, dtype):
    inside, outside = pl.BlockSpec(memory_space=pltpu.VMEM), pl.BlockSpec(memory_space=pl.ANY)
    return pl.pallas_call(
        kernel,
        out_shape=jax.ShapeDtypeStruct((2, depth, width), jnp.float32),
        in_specs=[outside] * n_outside + [inside] * (len(operands) - n_outside),
        out_specs=inside,
        scratch_shapes=[
            pltpu.VMEM((slots, 2, depth, depth), dtype),
            pltpu.VMEM((slots, 2, depth, width), dtype),
            pltpu.SemaphoreType.DMA((slots, 2)),
        ],
        compiler_params=pltpu.CompilerParams(vmem_limit_bytes=60 * 2**20),
        cost_estimate=pl.CostEstimate(flops=flops, bytes_accessed=n_outside * 2**20, transcendentals=0),
    )(*operands)


def per_device(slice_data):
    depth, width = slice_data.shape[1:]
    dtype = slice_data.dtype
    held = {(0, 0): slice_data, 0: slice_data}
    for i, (new, old, axis, hop) in enumerate(STEPS):
        value = held[old]
        if i >= WINDOW:
            past = STEPS[i - WINDOW][0]
            if past != old:
                value, held[past] = lax.optimization_barrier((value, held[past]))
        held[new] = move(value, axis, hop)

    unit = 8 * depth * depth * width
    early = [held[key] for key in list(NEAR) + EARLY]
    total = call(early_kernel, early, len(early), 2, unit * len(EARLY), depth, width, dtype)
    late = [held[key] for key in list(NEAR) + [4] + EARLY + LATE]
    kernel = functools.partial(late_kernel, 1.0 / float(NS) ** 0.5)
    return call(kernel, late + [total], len(late), len(LATE) + 2, unit * (len(LATE) + 2), depth, width, dtype)


def solution(mesh):
    in_specs = (P("freq", "rcv", "src"),)
    out_specs = P("freq", "rcv", "src")
    return jax.shard_map(
        per_device, mesh=mesh, in_specs=in_specs, out_specs=out_specs, check_vma=False
    )
```

time: 283 us -> 146 us (0.52)
  waiting for transfers between devices: 237 us -> 74.4 us
  starting transfers between devices: 0.04 us -> 39.6 us
  Pallas kernels: 0 us -> 30.6 us
  matrix products: 27.1 us -> 0 us
  between operations: 13.4 us -> 0.37 us
    all_gather x2 -> x0, waiting for transfers between devices: 235 us -> none  [the longest x1 129 us: per_device(): piece = lax.all_gather(slice_data, 'rcv', axis=1, tiled=True)]
    ppermute x0 -> x22, waiting for transfers between devices: none -> 74.4 us  [the longest x15 37.7 us: move(): return lax.ppermute(value, ('rcv', 'freq'), plane_pairs(axis == 'a', hop))]
    ppermute x0 -> x22, starting transfers between devices: none -> 39.6 us  [the longest x15 23.6 us: move(): return lax.ppermute(value, ('rcv', 'freq'), plane_pairs(axis == 'a', hop))]
    pallas_call x0 -> x2, Pallas kernels: none -> 30.6 us  [call(): pl.pallas_call(kernel, out_shape=jax.ShapeDtypeStruct((2, depth, width),...]
    dot_general x4 -> x0, matrix products: 27.1 us -> none  [the longest x1 8.65 us: per_device(): jnp.dot(left_im, right_re, preferred_element_type=jnp.float32)]
  transfers between devices with their start and end apart: 2 -> 22, of which waited for: 2 -> 6; matrix products, arithmetic and copies ran while one was open for 0% -> 0% of each run, Pallas kernels for 0% -> 13%
where the time goes in v1:
time: 146 us
  waiting for transfers between devices  74.4 us (51%)
  starting transfers between devices  39.6 us (27%)
  Pallas kernels  30.6 us (21%)
    ppermute x15, waiting for transfers between devices, move(): return lax.ppermute(value, ('rcv', 'freq'), plane_pairs(axis == 'a', hop))  37.7 us
    ppermute x7, waiting for transfers between devices, move(): return lax.ppermute(value, ('src', 'freq'), ring_pairs(hop))  36.8 us
    pallas_call x2, Pallas kernels, call(): pl.pallas_call(kernel, out_shape=jax.ShapeDtypeStruct((2, depth, width),...  30.6 us
    ppermute x15, starting transfers between devices, move(): return lax.ppermute(value, ('rcv', 'freq'), plane_pairs(axis == 'a', hop))  23.6 us
    ppermute x7, starting transfers between devices, move(): return lax.ppermute(value, ('src', 'freq'), ring_pairs(hop))  16 us
  transfers between devices with their start and end apart: 22, of which 6 were waited for; matrix products, arithmetic and copies ran while one was open for 0% of the time, Pallas kernels for 13%

profile of v1, /device:TPU:96, one launch (start us, length us, event | category | flops | bytes accessed | tf_op | source)
XLA Modules:
  0.0 146.0 jit_solution(14150417519774420748)
XLA Ops:
  0.0 1.5 %collective-permute-start.1 = (bf16[2,384,768]{2,1,0:T(8,128)(2,1)}, bf16[2,384,768]{2,1,0:T(8,128)(2,1)S(1)}, u32[]{:S(2)}, u32[]{:S(2)}) collective-permute-start(bf16[2,384,768]{2,1,0:T(8,128)(2,1)} %refs_8_.1), channel_id=1, source_target_pairs={{0,16},{1,65},{16,32},{17,81},{32,48},{33,97},{48,0},{49,113},{64,... | collective-permute-start | bytes 3538952 | tf_op jit(solution)/shard_map/ppermute | solution.py:63
  1.5 1.7 %collective-permute-start = (bf16[2,384,768]{2,1,0:T(8,128)(2,1)}, bf16[2,384,768]{2,1,0:T(8,128)(2,1)S(1)}, u32[]{:S(2)}, u32[]{:S(2)}) collective-permute-start(bf16[2,384,768]{2,1,0:T(8,128)(2,1)} %refs_8_.1), channel_id=1, source_target_pairs={{0,48},{1,193},{16,0},{17,209},{32,16},{33,225},{48,32},{49,241},{... | collective-permute-start | bytes 3538952 | tf_op jit(solution)/shard_map/ppermute | solution.py:63
  3.2 3.1 %collective-permute-start.3 = (bf16[2,384,768]{2,1,0:T(8,128)(2,1)}, bf16[2,384,768]{2,1,0:T(8,128)(2,1)S(1)}, u32[]{:S(2)}, u32[]{:S(2)}) collective-permute-start(bf16[2,384,768]{2,1,0:T(8,128)(2,1)} %refs_8_.1), channel_id=1, source_target_pairs={{0,2},{1,15},{2,4},{3,1},{4,6},{5,3},{6,8},{7,5},{8,10},{9,7},{10,... | collective-permute-start | bytes 3538952 | tf_op jit(solution)/shard_map/ppermute | solution.py:62
  6.4 11.3 %collective-permute-done.1.refs_8_.refs_9_ = bf16[2,384,768]{2,1,0:T(8,128)(2,1)S(1)} collective-permute-done((bf16[2,384,768]{2,1,0:T(8,128)(2,1)}, bf16[2,384,768]{2,1,0:T(8,128)(2,1)S(1)}, u32[]{:S(2)}, u32[]{:S(2)}) %collective-permute-start.1) | collective-permute-done | bytes 1179680 | tf_op jit(solution)/shard_map/ppermute | solution.py:63
  17.6 0.0 copy-start
  17.6 0.3 collective-permute-start.4
  17.9 3.0 %collective-permute-start.11 = (bf16[2,384,768]{2,1,0:T(8,128)(2,1)}, bf16[2,384,768]{2,1,0:T(8,128)(2,1)S(1)}, u32[]{:S(2)}, u32[]{:S(2)}) collective-permute-start(bf16[2,384,768]{2,1,0:T(8,128)(2,1)} %refs_8_.1), channel_id=1, source_target_pairs={{0,192},{1,49},{16,208},{17,1},{32,224},{33,17},{48,240},{49,33},{... | collective-permute-start | bytes 3538952 | tf_op jit(solution)/shard_map/ppermute | solution.py:63
  20.9 0.1 collective-permute-start.2
  21.0 0.0 collective-permute-done.refs_9_.refs_10_
  21.0 0.0 copy-start.1
  21.0 0.0 collective-permute-start.5
  21.0 0.0 collective-permute-done.3.refs_6_
  21.1 0.0 copy-start.2
  21.1 3.2 %collective-permute-start.7 = (bf16[2,384,768]{2,1,0:T(8,128)(2,1)S(1)}, bf16[2,384,768]{2,1,0:T(8,128)(2,1)S(1)}, u32[]{:S(2)}, u32[]{:S(2)}) collective-permute-start(bf16[2,384,768]{2,1,0:T(8,128)(2,1)S(1)} %collective-permute-done.1.refs_8_.refs_9_), channel_id=1, source_target_pairs={{0,192},{1,49},{16,208},{17,1},{32,224},{33,17},{48,240},{49,33},{... | collective-permute-start | bytes 3538952 | tf_op jit(solution)/shard_map/ppermute | solution.py:63
  24.3 19.7 %collective-permute-done.4.refs_10_.refs_11_ = bf16[2,384,768]{2,1,0:T(8,128)(2,1)S(1)} collective-permute-done((bf16[2,384,768]{2,1,0:T(8,128)(2,1)S(1)}, bf16[2,384,768]{2,1,0:T(8,128)(2,1)S(1)}, u32[]{:S(2)}, u32[]{:S(2)}) %collective-permute-start.4) | collective-permute-done | bytes 1179680 | tf_op jit(solution)/shard_map/ppermute | solution.py:63
  44.0 5.2 %collective-permute-start.12 = (bf16[2,384,768]{2,1,0:T(8,128)(2,1)S(1)}, bf16[2,384,768]{2,1,0:T(8,128)(2,1)S(1)}, u32[]{:S(2)}, u32[]{:S(2)}) collective-permute-start(bf16[2,384,768]{2,1,0:T(8,128)(2,1)S(1)} %collective-permute-done.3.refs_6_), channel_id=1, source_target_pairs={{0,2},{1,15},{2,4},{3,1},{4,6},{5,3},{6,8},{7,5},{8,10},{9,7},{10,... | collective-permute-start | bytes 3538952 | tf_op jit(solution)/shard_map/ppermute | solution.py:62
  49.2 0.0 collective-permute-done.11.refs_11_.refs_12_
  49.2 1.6 %collective-permute-start.13 = (bf16[2,384,768]{2,1,0:T(8,128)(2,1)S(1)}, bf16[2,384,768]{2,1,0:T(8,128)(2,1)}, u32[]{:S(2)}, u32[]{:S(2)}) collective-permute-start(bf16[2,384,768]{2,1,0:T(8,128)(2,1)S(1)} %collective-permute-done.1.refs_8_.refs_9_), channel_id=1, source_target_pairs={{0,64},{1,17},{16,80},{17,33},{32,96},{33,49},{48,112},{49,1},{64,... | collective-permute-start | bytes 3538952 | tf_op jit(solution)/shard_map/ppermute | solution.py:63
  50.8 0.0 collective-permute-done.2.refs_1_
  50.8 1.7 %collective-permute-start.10 = (bf16[2,384,768]{2,1,0:T(8,128)(2,1)S(1)}, bf16[2,384,768]{2,1,0:T(8,128)(2,1)}, u32[]{:S(2)}, u32[]{:S(2)}) collective-permute-start(bf16[2,384,768]{2,1,0:T(8,128)(2,1)S(1)} %collective-permute-done.refs_9_.refs_10_), channel_id=1, source_target_pairs={{0,192},{1,49},{16,208},{17,1},{32,224},{33,17},{48,240},{49,33},{... | collective-permute-start | bytes 3538952 | tf_op jit(solution)/shard_map/ppermute | solution.py:63
  52.5 0.0 collective-permute-done.5.refs_12_.refs_13_
  52.5 0.0 collective-permute-start.6
  52.5 0.0 collective-permute-done.7.refs_13_.refs_14_
  52.5 0.0 copy-start.7
  52.5 0.4 collective-permute-start.8
  52.9 22.3 %collective-permute-done.12.refs_5_ = bf16[2,384,768]{2,1,0:T(8,128)(2,1)S(1)} collective-permute-done((bf16[2,384,768]{2,1,0:T(8,128)(2,1)S(1)}, bf16[2,384,768]{2,1,0:T(8,128)(2,1)S(1)}, u32[]{:S(2)}, u32[]{:S(2)}) %collective-permute-start.12) | collective-permute-done | bytes 1179680 | tf_op jit(solution)/shard_map/ppermute | solution.py:62
  75.2 2.9 %collective-permute-start.17 = (bf16[2,384,768]{2,1,0:T(8,128)(2,1)S(1)}, bf16[2,384,768]{2,1,0:T(8,128)(2,1)S(1)}, u32[]{:S(2)}, u32[]{:S(2)}) collective-permute-start(bf16[2,384,768]{2,1,0:T(8,128)(2,1)S(1)} %collective-permute-done.11.refs_11_.refs_12_), channel_id=1, source_target_pairs={{0,192},{1,49},{16,208},{17,1},{32,224},{33,17},{48,240},{49,33},{... | collective-permute-start | bytes 3538952 | tf_op jit(solution)/shard_map/ppermute | solution.py:63
  78.1 0.0 collective-permute-done.13.refs_14_.refs_15_
  78.1 3.7 %collective-permute-start.14 = (bf16[2,384,768]{2,1,0:T(8,128)(2,1)S(1)}, bf16[2,384,768]{2,1,0:T(8,128)(2,1)}, u32[]{:S(2)}, u32[]{:S(2)}) collective-permute-start(bf16[2,384,768]{2,1,0:T(8,128)(2,1)S(1)} %collective-permute-done.12.refs_5_), channel_id=1, source_target_pairs={{0,2},{1,15},{2,4},{3,1},{4,6},{5,3},{6,8},{7,5},{8,10},{9,7},{10,... | collective-permute-start | bytes 3538952 | tf_op jit(solution)/shard_map/ppermute | solution.py:62
  81.8 0.0 collective-permute-done.10.refs_15_.refs_16_
  81.8 0.0 collective-permute-start.15
  81.8 0.0 collective-permute-done.6.refs_2_
  81.8 0.0 copy-start.9
  81.8 3.2 %collective-permute-start.18 = (bf16[2,384,768]{2,1,0:T(8,128)(2,1)S(1)}, bf16[2,384,768]{2,1,0:T(8,128)(2,1)S(1)}, u32[]{:S(2)}, u32[]{:S(2)}) collective-permute-start(bf16[2,384,768]{2,1,0:T(8,128)(2,1)S(1)} %collective-permute-done.4.refs_10_.refs_11_), channel_id=1, source_target_pairs={{0,192},{1,49},{16,208},{17,1},{32,224},{33,17},{48,240},{49,33},{... | collective-permute-start | bytes 3538952 | tf_op jit(solution)/shard_map/ppermute | solution.py:63
  85.0 0.0 collective-permute-done.8.refs_16_.refs_17_
  85.0 0.0 copy-done.3
  85.0 0.1 collective-permute-start.9
  85.1 6.7 %collective-permute-done.17.refs_17_.refs_18_ = bf16[2,384,768]{2,1,0:T(8,128)(2,1)S(1)} collective-permute-done((bf16[2,384,768]{2,1,0:T(8,128)(2,1)S(1)}, bf16[2,384,768]{2,1,0:T(8,128)(2,1)S(1)}, u32[]{:S(2)}, u32[]{:S(2)}) %collective-permute-start.17) | collective-permute-done | bytes 1179680 | tf_op jit(solution)/shard_map/ppermute | solution.py:63
  91.8 1.3 collective-permute-start.19
  93.1 12.5 %collective-permute-done.14.refs_4_ = bf16[2,384,768]{2,1,0:T(8,128)(2,1)} collective-permute-done((bf16[2,384,768]{2,1,0:T(8,128)(2,1)S(1)}, bf16[2,384,768]{2,1,0:T(8,128)(2,1)}, u32[]{:S(2)}, u32[]{:S(2)}) %collective-permute-start.14) | collective-permute-done | bytes 1179680 | tf_op jit(solution)/shard_map/ppermute | solution.py:62
  105.6 2.7 %collective-permute-start.20 = (bf16[2,384,768]{2,1,0:T(8,128)(2,1)}, bf16[2,384,768]{2,1,0:T(8,128)(2,1)}, u32[]{:S(2)}, u32[]{:S(2)}) collective-permute-start(bf16[2,384,768]{2,1,0:T(8,128)(2,1)} %collective-permute-done.10.refs_15_.refs_16_), channel_id=1, source_target_pairs={{0,192},{1,49},{16,208},{17,1},{32,224},{33,17},{48,240},{49,33},{... | collective-permute-start | bytes 3538952 | tf_op jit(solution)/shard_map/ppermute | solution.py:63
  108.2 0.0 collective-permute-done.15.refs_18_.refs_19_
  108.2 3.8 %collective-permute-start.16 = (bf16[2,384,768]{2,1,0:T(8,128)(2,1)}, bf16[2,384,768]{2,1,0:T(8,128)(2,1)}, u32[]{:S(2)}, u32[]{:S(2)}) collective-permute-start(bf16[2,384,768]{2,1,0:T(8,128)(2,1)} %collective-permute-done.14.refs_4_), channel_id=1, source_target_pairs={{0,2},{1,15},{2,4},{3,1},{4,6},{5,3},{6,8},{7,5},{8,10},{9,7},{10,... | collective-permute-start | bytes 3538952 | tf_op jit(solution)/shard_map/ppermute | solution.py:62
  112.0 0.0 collective-permute-done.18.refs_19_.refs_20_
  112.0 0.0 copy-done.4
  112.0 0.1 collective-permute-start.21
  112.1 0.0 copy-done.5
  112.1 0.0 copy-done.6
  112.2 0.0 copy-done.7
  112.2 0.0 copy-done.8
  112.2 0.0 copy-done.9
  112.2 0.0 copy-done.10
  112.2 0.0 copy-done.11
  112.2 0.9 copy-done.12
  113.1 2.0 %collective-permute-done.9.refs_3_ = bf16[2,384,768]{2,1,0:T(8,128)(2,1)} collective-permute-done((bf16[2,384,768]{2,1,0:T(8,128)(2,1)S(1)}, bf16[2,384,768]{2,1,0:T(8,128)(2,1)}, u32[]{:S(2)}, u32[]{:S(2)}) %collective-permute-start.9) | collective-permute-done | bytes 1179680 | tf_op jit(solution)/shard_map/ppermute | solution.py:62
  115.1 0.0 copy-done
  115.1 0.0 copy-done.1
  115.1 0.0 copy-done.2
  115.1 19.2 %shard_map.17.refs_24_ = f32[2,384,768]{2,1,0:T(8,128)} custom-call(bf16[2,384,768]{2,1,0:T(8,128)(2,1)} %refs_8_.1, bf16[2,384,768]{2,1,0:T(8,128)(2,1)} %copy-done.5, bf16[2,384,768]{2,1,0:T(8,128)(2,1)} %copy-done.9, bf16[2,384,768]{2,1,0:T(8,128)(2,1)} %collective-permute-done.9.refs_3_, bf16[2,384,768]{2,1,0:T(8,128)(2,1)} %collective-permute-done.14.refs_4_, ...), custom_call_target="tpu_custom_call" | custom-call | flops 11777605632 | bytes 20971520 | tf_op jit(solution)/shard_map/pallas_call | solution.py:189
  134.4 0.0 collective-permute-done.19.refs_21_
  134.4 0.0 collective-permute-done.20.refs_22_
  134.4 0.0 collective-permute-done.16.refs_7_
  134.4 0.0 collective-permute-done.21.refs_23_
  134.4 11.4 %shard_map.18 = f32[2,384,768]{2,1,0:T(8,128)} custom-call(bf16[2,384,768]{2,1,0:T(8,128)(2,1)} %refs_8_.1, bf16[2,384,768]{2,1,0:T(8,128)(2,1)} %copy-done.5, bf16[2,384,768]{2,1,0:T(8,128)(2,1)} %copy-done.9, bf16[2,384,768]{2,1,0:T(8,128)(2,1)} %collective-permute-done.9.refs_3_, bf16[2,384,768]{2,1,0:T(8,128)(2,1)} %collective-permute-done.14.refs_4_, ...), custom_call_target="tpu_custom_call" | custom-call | flops 4529848320 | bytes 25165824 | tf_op jit(solution)/shard_map/pallas_call | solution.py:189
  (8 shorter events, 0.0 us)
Async XLA Ops:
  0.0 17.6 %collective-permute-start.1 = (bf16[2,384,768]{2,1,0:T(8,128)(2,1)}, bf16[2,384,768]{2,1,0:T(8,128)(2,1)S(1)}, u32[]{:S(2)}, u32[]{:S(2)}) collective-permute-start(bf16[2,384,768]{2,1,0:T(8,128)(2,1)} %refs_8_.1), channel_id=1, source_target_pairs={{0,16},{1,65},{16,32},{17,81},{32,48},{33,97},{48,0},{49,113},{64,... | collective-permute-start | bytes 3538952 | tf_op jit(solution)/shard_map/ppermute | solution.py:63
  1.5 19.5 %collective-permute-start = (bf16[2,384,768]{2,1,0:T(8,128)(2,1)}, bf16[2,384,768]{2,1,0:T(8,128)(2,1)S(1)}, u32[]{:S(2)}, u32[]{:S(2)}) collective-permute-start(bf16[2,384,768]{2,1,0:T(8,128)(2,1)} %refs_8_.1), channel_id=1, source_target_pairs={{0,48},{1,193},{16,0},{17,209},{32,16},{33,225},{48,32},{49,241},{... | collective-permute-start | bytes 3538952 | tf_op jit(solution)/shard_map/ppermute | solution.py:63
  3.2 17.8 %collective-permute-start.3 = (bf16[2,384,768]{2,1,0:T(8,128)(2,1)}, bf16[2,384,768]{2,1,0:T(8,128)(2,1)S(1)}, u32[]{:S(2)}, u32[]{:S(2)}) collective-permute-start(bf16[2,384,768]{2,1,0:T(8,128)(2,1)} %refs_8_.1), channel_id=1, source_target_pairs={{0,2},{1,15},{2,4},{3,1},{4,6},{5,3},{6,8},{7,5},{8,10},{9,7},{10,... | collective-permute-start | bytes 3538952 | tf_op jit(solution)/shard_map/ppermute | solution.py:62
  17.6 97.5 %copy-start = (bf16[2,384,768]{2,1,0:T(8,128)(2,1)}, bf16[2,384,768]{2,1,0:T(8,128)(2,1)S(1)}, u32[]{:S(2)}) copy-start(bf16[2,384,768]{2,1,0:T(8,128)(2,1)S(1)} %collective-permute-done.1.refs_8_.refs_9_) | copy-start | bytes 3538948
  17.6 26.3 %collective-permute-start.4 = (bf16[2,384,768]{2,1,0:T(8,128)(2,1)S(1)}, bf16[2,384,768]{2,1,0:T(8,128)(2,1)S(1)}, u32[]{:S(2)}, u32[]{:S(2)}) collective-permute-start(bf16[2,384,768]{2,1,0:T(8,128)(2,1)S(1)} %collective-permute-done.1.refs_8_.refs_9_), channel_id=1, source_target_pairs={{0,16},{1,65},{16,32},{17,81},{32,48},{33,97},{48,0},{49,113},{64,... | collective-permute-start | bytes 3538952 | tf_op jit(solution)/shard_map/ppermute | solution.py:63
  17.9 31.3 %collective-permute-start.11 = (bf16[2,384,768]{2,1,0:T(8,128)(2,1)}, bf16[2,384,768]{2,1,0:T(8,128)(2,1)S(1)}, u32[]{:S(2)}, u32[]{:S(2)}) collective-permute-start(bf16[2,384,768]{2,1,0:T(8,128)(2,1)} %refs_8_.1), channel_id=1, source_target_pairs={{0,192},{1,49},{16,208},{17,1},{32,224},{33,17},{48,240},{49,33},{... | collective-permute-start | bytes 3538952 | tf_op jit(solution)/shard_map/ppermute | solution.py:63
  20.9 29.9 %collective-permute-start.2 = (bf16[2,384,768]{2,1,0:T(8,128)(2,1)}, bf16[2,384,768]{2,1,0:T(8,128)(2,1)S(1)}, u32[]{:S(2)}, u32[]{:S(2)}) collective-permute-start(bf16[2,384,768]{2,1,0:T(8,128)(2,1)} %refs_8_.1), channel_id=1, source_target_pairs={{0,14},{1,3},{2,0},{3,5},{4,2},{5,7},{6,4},{7,9},{8,6},{9,11},{10,... | collective-permute-start | bytes 3538952 | tf_op jit(solution)/shard_map/ppermute | solution.py:62
  21.0 94.1 %copy-start.1 = (bf16[2,384,768]{2,1,0:T(8,128)(2,1)}, bf16[2,384,768]{2,1,0:T(8,128)(2,1)S(1)}, u32[]{:S(2)}) copy-start(bf16[2,384,768]{2,1,0:T(8,128)(2,1)S(1)} %collective-permute-done.refs_9_.refs_10_) | copy-start | bytes 3538948
  21.0 31.4 %collective-permute-start.5 = (bf16[2,384,768]{2,1,0:T(8,128)(2,1)}, bf16[2,384,768]{2,1,0:T(8,128)(2,1)S(1)}, u32[]{:S(2)}, u32[]{:S(2)}) collective-permute-start(bf16[2,384,768]{2,1,0:T(8,128)(2,1)} %refs_8_.1), channel_id=1, source_target_pairs={{0,64},{1,17},{16,80},{17,33},{32,96},{33,49},{48,112},{49,1},{64,... | collective-permute-start | bytes 3538952 | tf_op jit(solution)/shard_map/ppermute | solution.py:63
  21.1 94.1 %copy-start.2 = (bf16[2,384,768]{2,1,0:T(8,128)(2,1)}, bf16[2,384,768]{2,1,0:T(8,128)(2,1)S(1)}, u32[]{:S(2)}) copy-start(bf16[2,384,768]{2,1,0:T(8,128)(2,1)S(1)} %collective-permute-done.3.refs_6_) | copy-start | bytes 3538948
  21.1 31.4 %collective-permute-start.7 = (bf16[2,384,768]{2,1,0:T(8,128)(2,1)S(1)}, bf16[2,384,768]{2,1,0:T(8,128)(2,1)S(1)}, u32[]{:S(2)}, u32[]{:S(2)}) collective-permute-start(bf16[2,384,768]{2,1,0:T(8,128)(2,1)S(1)} %collective-permute-done.1.refs_8_.refs_9_), channel_id=1, source_target_pairs={{0,192},{1,49},{16,208},{17,1},{32,224},{33,17},{48,240},{49,33},{... | collective-permute-start | bytes 3538952 | tf_op jit(solution)/shard_map/ppermute | solution.py:63
  44.0 41.0 %copy-start.3 = (bf16[2,384,768]{2,1,0:T(8,128)(2,1)}, bf16[2,384,768]{2,1,0:T(8,128)(2,1)S(1)}, u32[]{:S(2)}) copy-start(bf16[2,384,768]{2,1,0:T(8,128)(2,1)S(1)} %collective-permute-done.4.refs_10_.refs_11_) | copy-start | bytes 3538948
  44.0 31.2 %collective-permute-start.12 = (bf16[2,384,768]{2,1,0:T(8,128)(2,1)S(1)}, bf16[2,384,768]{2,1,0:T(8,128)(2,1)S(1)}, u32[]{:S(2)}, u32[]{:S(2)}) collective-permute-start(bf16[2,384,768]{2,1,0:T(8,128)(2,1)S(1)} %collective-permute-done.3.refs_6_), channel_id=1, source_target_pairs={{0,2},{1,15},{2,4},{3,1},{4,6},{5,3},{6,8},{7,5},{8,10},{9,7},{10,... | collective-permute-start | bytes 3538952 | tf_op jit(solution)/shard_map/ppermute | solution.py:62
  49.2 62.8 %copy-start.4 = (bf16[2,384,768]{2,1,0:T(8,128)(2,1)}, bf16[2,384,768]{2,1,0:T(8,128)(2,1)S(1)}, u32[]{:S(2)}) copy-start(bf16[2,384,768]{2,1,0:T(8,128)(2,1)S(1)} %collective-permute-done.11.refs_11_.refs_12_) | copy-start | bytes 3538948
  49.2 28.9 %collective-permute-start.13 = (bf16[2,384,768]{2,1,0:T(8,128)(2,1)S(1)}, bf16[2,384,768]{2,1,0:T(8,128)(2,1)}, u32[]{:S(2)}, u32[]{:S(2)}) collective-permute-start(bf16[2,384,768]{2,1,0:T(8,128)(2,1)S(1)} %collective-permute-done.1.refs_8_.refs_9_), channel_id=1, source_target_pairs={{0,64},{1,17},{16,80},{17,33},{32,96},{33,49},{48,112},{49,1},{64,... | collective-permute-start | bytes 3538952 | tf_op jit(solution)/shard_map/ppermute | solution.py:63
  50.8 61.3 %copy-start.5 = (bf16[2,384,768]{2,1,0:T(8,128)(2,1)}, bf16[2,384,768]{2,1,0:T(8,128)(2,1)S(1)}, u32[]{:S(2)}) copy-start(bf16[2,384,768]{2,1,0:T(8,128)(2,1)S(1)} %collective-permute-done.2.refs_1_) | copy-start | bytes 3538948
  50.8 31.0 %collective-permute-start.10 = (bf16[2,384,768]{2,1,0:T(8,128)(2,1)S(1)}, bf16[2,384,768]{2,1,0:T(8,128)(2,1)}, u32[]{:S(2)}, u32[]{:S(2)}) collective-permute-start(bf16[2,384,768]{2,1,0:T(8,128)(2,1)S(1)} %collective-permute-done.refs_9_.refs_10_), channel_id=1, source_target_pairs={{0,192},{1,49},{16,208},{17,1},{32,224},{33,17},{48,240},{49,33},{... | collective-permute-start | bytes 3538952 | tf_op jit(solution)/shard_map/ppermute | solution.py:63
  52.5 59.7 %copy-start.6 = (bf16[2,384,768]{2,1,0:T(8,128)(2,1)}, bf16[2,384,768]{2,1,0:T(8,128)(2,1)S(1)}, u32[]{:S(2)}) copy-start(bf16[2,384,768]{2,1,0:T(8,128)(2,1)S(1)} %collective-permute-done.5.refs_12_.refs_13_) | copy-start | bytes 3538948
  52.5 29.3 %collective-permute-start.6 = (bf16[2,384,768]{2,1,0:T(8,128)(2,1)S(1)}, bf16[2,384,768]{2,1,0:T(8,128)(2,1)S(1)}, u32[]{:S(2)}, u32[]{:S(2)}) collective-permute-start(bf16[2,384,768]{2,1,0:T(8,128)(2,1)S(1)} %collective-permute-done.2.refs_1_), channel_id=1, source_target_pairs={{0,14},{1,3},{2,0},{3,5},{4,2},{5,7},{6,4},{7,9},{8,6},{9,11},{10,... | collective-permute-start | bytes 3538952 | tf_op jit(solution)/shard_map/ppermute | solution.py:62
  52.5 59.7 %copy-start.7 = (bf16[2,384,768]{2,1,0:T(8,128)(2,1)}, bf16[2,384,768]{2,1,0:T(8,128)(2,1)S(1)}, u32[]{:S(2)}) copy-start(bf16[2,384,768]{2,1,0:T(8,128)(2,1)S(1)} %collective-permute-done.7.refs_13_.refs_14_) | copy-start | bytes 3538948
  52.5 32.5 %collective-permute-start.8 = (bf16[2,384,768]{2,1,0:T(8,128)(2,1)S(1)}, bf16[2,384,768]{2,1,0:T(8,128)(2,1)S(1)}, u32[]{:S(2)}, u32[]{:S(2)}) collective-permute-start(bf16[2,384,768]{2,1,0:T(8,128)(2,1)S(1)} %collective-permute-done.refs_9_.refs_10_), channel_id=1, source_target_pairs={{0,64},{1,17},{16,80},{17,33},{32,96},{33,49},{48,112},{49,1},{64,... | collective-permute-start | bytes 3538952 | tf_op jit(solution)/shard_map/ppermute | solution.py:63
  75.2 37.0 %copy-start.8 = (bf16[2,384,768]{2,1,0:T(8,128)(2,1)}, bf16[2,384,768]{2,1,0:T(8,128)(2,1)S(1)}, u32[]{:S(2)}) copy-start(bf16[2,384,768]{2,1,0:T(8,128)(2,1)S(1)} %collective-permute-done.12.refs_5_) | copy-start | bytes 3538948
  75.2 16.6 %collective-permute-start.17 = (bf16[2,384,768]{2,1,0:T(8,128)(2,1)S(1)}, bf16[2,384,768]{2,1,0:T(8,128)(2,1)S(1)}, u32[]{:S(2)}, u32[]{:S(2)}) collective-permute-start(bf16[2,384,768]{2,1,0:T(8,128)(2,1)S(1)} %collective-permute-done.11.refs_11_.refs_12_), channel_id=1, source_target_pairs={{0,192},{1,49},{16,208},{17,1},{32,224},{33,17},{48,240},{49,33},{... | collective-permute-start | bytes 3538952 | tf_op jit(solution)/shard_map/ppermute | solution.py:63
  78.1 27.5 %collective-permute-start.14 = (bf16[2,384,768]{2,1,0:T(8,128)(2,1)S(1)}, bf16[2,384,768]{2,1,0:T(8,128)(2,1)}, u32[]{:S(2)}, u32[]{:S(2)}) collective-permute-start(bf16[2,384,768]{2,1,0:T(8,128)(2,1)S(1)} %collective-permute-done.12.refs_5_), channel_id=1, source_target_pairs={{0,2},{1,15},{2,4},{3,1},{4,6},{5,3},{6,8},{7,5},{8,10},{9,7},{10,... | collective-permute-start | bytes 3538952 | tf_op jit(solution)/shard_map/ppermute | solution.py:62
  81.8 26.5 %collective-permute-start.15 = (bf16[2,384,768]{2,1,0:T(8,128)(2,1)S(1)}, bf16[2,384,768]{2,1,0:T(8,128)(2,1)}, u32[]{:S(2)}, u32[]{:S(2)}) collective-permute-start(bf16[2,384,768]{2,1,0:T(8,128)(2,1)S(1)} %collective-permute-done.4.refs_10_.refs_11_), channel_id=1, source_target_pairs={{0,64},{1,17},{16,80},{17,33},{32,96},{33,49},{48,112},{49,1},{64,... | collective-permute-start | bytes 3538952 | tf_op jit(solution)/shard_map/ppermute | solution.py:63
  81.8 30.4 %copy-start.9 = (bf16[2,384,768]{2,1,0:T(8,128)(2,1)}, bf16[2,384,768]{2,1,0:T(8,128)(2,1)S(1)}, u32[]{:S(2)}) copy-start(bf16[2,384,768]{2,1,0:T(8,128)(2,1)S(1)} %collective-permute-done.6.refs_2_) | copy-start | bytes 3538948
  81.8 30.3 %collective-permute-start.18 = (bf16[2,384,768]{2,1,0:T(8,128)(2,1)S(1)}, bf16[2,384,768]{2,1,0:T(8,128)(2,1)S(1)}, u32[]{:S(2)}, u32[]{:S(2)}) collective-permute-start(bf16[2,384,768]{2,1,0:T(8,128)(2,1)S(1)} %collective-permute-done.4.refs_10_.refs_11_), channel_id=1, source_target_pairs={{0,192},{1,49},{16,208},{17,1},{32,224},{33,17},{48,240},{49,33},{... | collective-permute-start | bytes 3538952 | tf_op jit(solution)/shard_map/ppermute | solution.py:63
  85.0 27.2 %copy-start.10 = (bf16[2,384,768]{2,1,0:T(8,128)(2,1)}, bf16[2,384,768]{2,1,0:T(8,128)(2,1)S(1)}, u32[]{:S(2)}) copy-start(bf16[2,384,768]{2,1,0:T(8,128)(2,1)S(1)} %collective-permute-done.8.refs_16_.refs_17_) | copy-start | bytes 3538948
  85.0 30.1 %collective-permute-start.9 = (bf16[2,384,768]{2,1,0:T(8,128)(2,1)S(1)}, bf16[2,384,768]{2,1,0:T(8,128)(2,1)}, u32[]{:S(2)}, u32[]{:S(2)}) collective-permute-start(bf16[2,384,768]{2,1,0:T(8,128)(2,1)S(1)} %collective-permute-done.6.refs_2_), channel_id=1, source_target_pairs={{0,14},{1,3},{2,0},{3,5},{4,2},{5,7},{6,4},{7,9},{8,6},{9,11},{10,... | collective-permute-start | bytes 3538952 | tf_op jit(solution)/shard_map/ppermute | solution.py:62
  91.8 20.4 %copy-start.11 = (bf16[2,384,768]{2,1,0:T(8,128)(2,1)}, bf16[2,384,768]{2,1,0:T(8,128)(2,1)S(1)}, u32[]{:S(2)}) copy-start(bf16[2,384,768]{2,1,0:T(8,128)(2,1)S(1)} %collective-permute-done.17.refs_17_.refs_18_) | copy-start | bytes 3538948
  91.8 42.6 %collective-permute-start.19 = (bf16[2,384,768]{2,1,0:T(8,128)(2,1)}, bf16[2,384,768]{2,1,0:T(8,128)(2,1)}, u32[]{:S(2)}, u32[]{:S(2)}) collective-permute-start(bf16[2,384,768]{2,1,0:T(8,128)(2,1)} %collective-permute-done.13.refs_14_.refs_15_), channel_id=1, source_target_pairs={{0,64},{1,17},{16,80},{17,33},{32,96},{33,49},{48,112},{49,1},{64,... | collective-permute-start | bytes 3538952 | tf_op jit(solution)/shard_map/ppermute | solution.py:63
  105.6 28.8 %collective-permute-start.20 = (bf16[2,384,768]{2,1,0:T(8,128)(2,1)}, bf16[2,384,768]{2,1,0:T(8,128)(2,1)}, u32[]{:S(2)}, u32[]{:S(2)}) collective-permute-start(bf16[2,384,768]{2,1,0:T(8,128)(2,1)} %collective-permute-done.10.refs_15_.refs_16_), channel_id=1, source_target_pairs={{0,192},{1,49},{16,208},{17,1},{32,224},{33,17},{48,240},{49,33},{... | collective-permute-start | bytes 3538952 | tf_op jit(solution)/shard_map/ppermute | solution.py:63
  108.2 26.1 %collective-permute-start.16 = (bf16[2,384,768]{2,1,0:T(8,128)(2,1)}, bf16[2,384,768]{2,1,0:T(8,128)(2,1)}, u32[]{:S(2)}, u32[]{:S(2)}) collective-permute-start(bf16[2,384,768]{2,1,0:T(8,128)(2,1)} %collective-permute-done.14.refs_4_), channel_id=1, source_target_pairs={{0,2},{1,15},{2,4},{3,1},{4,6},{5,3},{6,8},{7,5},{8,10},{9,7},{10,... | collective-permute-start | bytes 3538952 | tf_op jit(solution)/shard_map/ppermute | solution.py:62
  112.0 1.1 copy-start.12
  112.0 22.3 %collective-permute-start.21 = (bf16[2,384,768]{2,1,0:T(8,128)(2,1)}, bf16[2,384,768]{2,1,0:T(8,128)(2,1)}, u32[]{:S(2)}, u32[]{:S(2)}) collective-permute-start(bf16[2,384,768]{2,1,0:T(8,128)(2,1)} %collective-permute-done.15.refs_18_.refs_19_), channel_id=1, source_target_pairs={{0,64},{1,17},{16,80},{17,33},{32,96},{33,49},{48,112},{49,1},{64,... | collective-permute-start | bytes 3538952 | tf_op jit(solution)/shard_map/ppermute | solution.py:63

commit v2 on v1

--- a/solution.py
+++ b/solution.py
@@ -109,9 +109,11 @@
     refs = list(refs)
     lefts = [refs.pop(0) for _ in NEAR]
     rights = [refs.pop(0) for _ in EARLY]
-    out, l_buf, r_buf, sems = refs
+    out, l_buf, r_buf, sems, flags = refs
     owners = [owner_of(key) for key in EARLY]
     ready = [left_code(owner) != 4 for owner in owners]
+    for k, hit in enumerate(ready):
+        flags[k] = hit.astype(jnp.int32)
 
     def start(k):
         @pl.when(ready[k])
@@ -121,15 +123,23 @@
 
     start(0)
     out[...] = jnp.zeros_like(out)
-    for k in range(len(EARLY)):
-        if k + 1 < len(EARLY):
-            start(k + 1)
-
-        @pl.when(ready[k])
-        def _():
-            pltpu.make_async_copy(rights[k], r_buf.at[k % 2], sems.at[k % 2, 0]).wait()
-            pltpu.make_async_copy(lefts[0].at[:, :, pl.ds(0, l_buf.shape[-1])], l_buf.at[k % 2], sems.at[k % 2, 1]).wait()
-            out[...] += product(l_buf[k % 2], r_buf[k % 2])
+
+    def step(k, carry):
+        for j in range(1, len(EARLY)):
+            @pl.when(k + 1 == j)
+            def _():
+                start(j)
+
+        @pl.when(flags[k] == 1)
+        def _():
+            slot = lax.rem(k, 2)
+            pltpu.make_async_copy(rights[0], r_buf.at[slot], sems.at[slot, 0]).wait()
+            pltpu.make_async_copy(lefts[0].at[:, :, pl.ds(0, l_buf.shape[-1])], l_buf.at[slot], sems.at[slot, 1]).wait()
+            out[...] += product(l_buf[slot], r_buf[slot])
+
+        return carry
+
+    lax.fori_loop(0, len(EARLY), step, 0)
 
 
 def late_kernel(scale, *refs):
@@ -137,7 +147,7 @@
     keys = NEAR + (4,)
     lefts = [refs.pop(0) for _ in keys]
     rights = [refs.pop(0) for _ in EARLY + LATE]
-    total, out, l_buf, r_buf, sems = refs
+    total, out, l_buf, r_buf, sems, flags = refs
     here = lax.axis_index("src")
     depth = l_buf.shape[-1]
     tasks = []
@@ -166,21 +176,21 @@
             start = pl.multiple_of((owner % 2) * depth, depth)
             pltpu.make_async_copy(lefts[-1].at[:, :, pl.ds(start, depth)], l_buf.at[k], sems.at[k, 1]).start()
 
-    def finish(k, right=True):
+    for k, (_, code) in enumerate(tasks):
+        flags[k] = 1 if code is None else is_early(code).astype(jnp.int32)
+    out[...] = total[...]
+
+    def step(k, carry):
         pltpu.make_async_copy(lefts[0].at[:, :, pl.ds(0, depth)], l_buf.at[k], sems.at[k, 1]).wait()
 
-    out[...] = total[...]
-    for k, (owner, code) in enumerate(tasks):
-        pltpu.make_async_copy(lefts[0].at[:, :, pl.ds(0, depth)], l_buf.at[k], sems.at[k, 1]).wait()
-
-        def work():
+        @pl.when(flags[k] == 1)
+        def _():
             pltpu.make_async_copy(rights[0], r_buf.at[k], sems.at[k, 0]).wait()
             out[...] += product(l_buf[k], r_buf[k])
 
-        if code is None:
-            work()
-        else:
-            pl.when(is_early(code))(work)
+        return carry
+
+    lax.fori_loop(0, len(tasks), step, 0)
     out[...] *= scale
 
 
@@ -195,6 +205,7 @@
             pltpu.VMEM((slots, 2, depth, depth), dtype),
             pltpu.VMEM((slots, 2, depth, width), dtype),
             pltpu.SemaphoreType.DMA((slots, 2)),
+            pltpu.SMEM((16,), jnp.int32),
         ],
         compiler_params=pltpu.CompilerParams(vmem_limit_bytes=60 * 2**20),
         cost_estimate=pl.CostEstimate(flops=flops, bytes_accessed=n_outside * 2**20, transcendentals=0),

time: 146 us -> 146 us (level)
  transfers between devices with their start and end apart: 22 -> 22, of which waited for: 6 -> 6; matrix products, arithmetic and copies ran while one was open for 0% -> 0% of each run, Pallas kernels for 13% -> 14%
where the time goes in v2:
time: 146 us; the launch traced here: 145 us
  waiting for transfers between devices  74.4 us (51%)
  starting transfers between devices  39.6 us (27%)
  Pallas kernels  30.1 us (21%)
    ppermute x15, waiting for transfers between devices, move(): return lax.ppermute(value, ('rcv', 'freq'), plane_pairs(axis == 'a', hop))  37.7 us
    ppermute x7, waiting for transfers between devices, move(): return lax.ppermute(value, ('src', 'freq'), ring_pairs(hop))  36.8 us
    pallas_call x2, Pallas kernels, call(): pl.pallas_call(kernel, out_shape=jax.ShapeDtypeStruct((2, depth, width),...  30.1 us
    ppermute x15, starting transfers between devices, move(): return lax.ppermute(value, ('rcv', 'freq'), plane_pairs(axis == 'a', hop))  23.6 us
    ppermute x7, starting transfers between devices, move(): return lax.ppermute(value, ('src', 'freq'), ring_pairs(hop))  16 us
  transfers between devices with their start and end apart: 22, of which 6 were waited for; matrix products, arithmetic and copies ran while one was open for 0% of the time, Pallas kernels for 14%

profile of v2, /device:TPU:96, one launch (start us, length us, event | category | flops | bytes accessed | tf_op | source)
XLA Modules:
  0.0 145.4 jit_solution(12239995015557408656)
XLA Ops:
  0.0 1.5 %collective-permute-start.1 = (bf16[2,384,768]{2,1,0:T(8,128)(2,1)}, bf16[2,384,768]{2,1,0:T(8,128)(2,1)S(1)}, u32[]{:S(2)}, u32[]{:S(2)}) collective-permute-start(bf16[2,384,768]{2,1,0:T(8,128)(2,1)} %refs_8_.1), channel_id=1, source_target_pairs={{0,16},{1,65},{16,32},{17,81},{32,48},{33,97},{48,0},{49,113},{64,... | collective-permute-start | bytes 3538952 | tf_op jit(solution)/shard_map/ppermute | solution.py:63
  1.5 1.7 %collective-permute-start = (bf16[2,384,768]{2,1,0:T(8,128)(2,1)}, bf16[2,384,768]{2,1,0:T(8,128)(2,1)S(1)}, u32[]{:S(2)}, u32[]{:S(2)}) collective-permute-start(bf16[2,384,768]{2,1,0:T(8,128)(2,1)} %refs_8_.1), channel_id=1, source_target_pairs={{0,48},{1,193},{16,0},{17,209},{32,16},{33,225},{48,32},{49,241},{... | collective-permute-start | bytes 3538952 | tf_op jit(solution)/shard_map/ppermute | solution.py:63
  3.2 3.1 %collective-permute-start.3 = (bf16[2,384,768]{2,1,0:T(8,128)(2,1)}, bf16[2,384,768]{2,1,0:T(8,128)(2,1)S(1)}, u32[]{:S(2)}, u32[]{:S(2)}) collective-permute-start(bf16[2,384,768]{2,1,0:T(8,128)(2,1)} %refs_8_.1), channel_id=1, source_target_pairs={{0,2},{1,15},{2,4},{3,1},{4,6},{5,3},{6,8},{7,5},{8,10},{9,7},{10,... | collective-permute-start | bytes 3538952 | tf_op jit(solution)/shard_map/ppermute | solution.py:62
  6.4 11.3 %collective-permute-done.1.refs_8_.refs_9_ = bf16[2,384,768]{2,1,0:T(8,128)(2,1)S(1)} collective-permute-done((bf16[2,384,768]{2,1,0:T(8,128)(2,1)}, bf16[2,384,768]{2,1,0:T(8,128)(2,1)S(1)}, u32[]{:S(2)}, u32[]{:S(2)}) %collective-permute-start.1) | collective-permute-done | bytes 1179680 | tf_op jit(solution)/shard_map/ppermute | solution.py:63
  17.6 0.0 copy-start
  17.6 0.3 collective-permute-start.4
  17.9 3.0 %collective-permute-start.11 = (bf16[2,384,768]{2,1,0:T(8,128)(2,1)}, bf16[2,384,768]{2,1,0:T(8,128)(2,1)S(1)}, u32[]{:S(2)}, u32[]{:S(2)}) collective-permute-start(bf16[2,384,768]{2,1,0:T(8,128)(2,1)} %refs_8_.1), channel_id=1, source_target_pairs={{0,192},{1,49},{16,208},{17,1},{32,224},{33,17},{48,240},{49,33},{... | collective-permute-start | bytes 3538952 | tf_op jit(solution)/shard_map/ppermute | solution.py:63
  20.9 0.1 collective-permute-start.2
  21.0 0.0 collective-permute-done.refs_9_.refs_10_
  21.0 0.0 copy-start.1
  21.0 0.0 collective-permute-start.5
  21.0 0.0 collective-permute-done.3.refs_6_
  21.1 0.0 copy-start.2
  21.1 3.2 %collective-permute-start.7 = (bf16[2,384,768]{2,1,0:T(8,128)(2,1)S(1)}, bf16[2,384,768]{2,1,0:T(8,128)(2,1)S(1)}, u32[]{:S(2)}, u32[]{:S(2)}) collective-permute-start(bf16[2,384,768]{2,1,0:T(8,128)(2,1)S(1)} %collective-permute-done.1.refs_8_.refs_9_), channel_id=1, source_target_pairs={{0,192},{1,49},{16,208},{17,1},{32,224},{33,17},{48,240},{49,33},{... | collective-permute-start | bytes 3538952 | tf_op jit(solution)/shard_map/ppermute | solution.py:63
  24.3 19.7 %collective-permute-done.4.refs_10_.refs_11_ = bf16[2,384,768]{2,1,0:T(8,128)(2,1)S(1)} collective-permute-done((bf16[2,384,768]{2,1,0:T(8,128)(2,1)S(1)}, bf16[2,384,768]{2,1,0:T(8,128)(2,1)S(1)}, u32[]{:S(2)}, u32[]{:S(2)}) %collective-permute-start.4) | collective-permute-done | bytes 1179680 | tf_op jit(solution)/shard_map/ppermute | solution.py:63
  44.0 5.2 %collective-permute-start.12 = (bf16[2,384,768]{2,1,0:T(8,128)(2,1)S(1)}, bf16[2,384,768]{2,1,0:T(8,128)(2,1)S(1)}, u32[]{:S(2)}, u32[]{:S(2)}) collective-permute-start(bf16[2,384,768]{2,1,0:T(8,128)(2,1)S(1)} %collective-permute-done.3.refs_6_), channel_id=1, source_target_pairs={{0,2},{1,15},{2,4},{3,1},{4,6},{5,3},{6,8},{7,5},{8,10},{9,7},{10,... | collective-permute-start | bytes 3538952 | tf_op jit(solution)/shard_map/ppermute | solution.py:62
  49.2 0.0 collective-permute-done.11.refs_11_.refs_12_
  49.2 1.6 %collective-permute-start.13 = (bf16[2,384,768]{2,1,0:T(8,128)(2,1)S(1)}, bf16[2,384,768]{2,1,0:T(8,128)(2,1)}, u32[]{:S(2)}, u32[]{:S(2)}) collective-permute-start(bf16[2,384,768]{2,1,0:T(8,128)(2,1)S(1)} %collective-permute-done.1.refs_8_.refs_9_), channel_id=1, source_target_pairs={{0,64},{1,17},{16,80},{17,33},{32,96},{33,49},{48,112},{49,1},{64,... | collective-permute-start | bytes 3538952 | tf_op jit(solution)/shard_map/ppermute | solution.py:63
  50.8 0.0 collective-permute-done.2.refs_1_
  50.8 1.7 %collective-permute-start.10 = (bf16[2,384,768]{2,1,0:T(8,128)(2,1)S(1)}, bf16[2,384,768]{2,1,0:T(8,128)(2,1)}, u32[]{:S(2)}, u32[]{:S(2)}) collective-permute-start(bf16[2,384,768]{2,1,0:T(8,128)(2,1)S(1)} %collective-permute-done.refs_9_.refs_10_), channel_id=1, source_target_pairs={{0,192},{1,49},{16,208},{17,1},{32,224},{33,17},{48,240},{49,33},{... | collective-permute-start | bytes 3538952 | tf_op jit(solution)/shard_map/ppermute | solution.py:63
  52.5 0.0 collective-permute-done.5.refs_12_.refs_13_
  52.5 0.0 collective-permute-start.6
  52.5 0.0 collective-permute-done.7.refs_13_.refs_14_
  52.5 0.0 copy-start.7
  52.5 0.4 collective-permute-start.8
  52.9 22.3 %collective-permute-done.12.refs_5_ = bf16[2,384,768]{2,1,0:T(8,128)(2,1)S(1)} collective-permute-done((bf16[2,384,768]{2,1,0:T(8,128)(2,1)S(1)}, bf16[2,384,768]{2,1,0:T(8,128)(2,1)S(1)}, u32[]{:S(2)}, u32[]{:S(2)}) %collective-permute-start.12) | collective-permute-done | bytes 1179680 | tf_op jit(solution)/shard_map/ppermute | solution.py:62
  75.2 2.9 %collective-permute-start.17 = (bf16[2,384,768]{2,1,0:T(8,128)(2,1)S(1)}, bf16[2,384,768]{2,1,0:T(8,128)(2,1)S(1)}, u32[]{:S(2)}, u32[]{:S(2)}) collective-permute-start(bf16[2,384,768]{2,1,0:T(8,128)(2,1)S(1)} %collective-permute-done.11.refs_11_.refs_12_), channel_id=1, source_target_pairs={{0,192},{1,49},{16,208},{17,1},{32,224},{33,17},{48,240},{49,33},{... | collective-permute-start | bytes 3538952 | tf_op jit(solution)/shard_map/ppermute | solution.py:63
  78.1 0.0 collective-permute-done.13.refs_14_.refs_15_
  78.1 3.7 %collective-permute-start.14 = (bf16[2,384,768]{2,1,0:T(8,128)(2,1)S(1)}, bf16[2,384,768]{2,1,0:T(8,128)(2,1)}, u32[]{:S(2)}, u32[]{:S(2)}) collective-permute-start(bf16[2,384,768]{2,1,0:T(8,128)(2,1)S(1)} %collective-permute-done.12.refs_5_), channel_id=1, source_target_pairs={{0,2},{1,15},{2,4},{3,1},{4,6},{5,3},{6,8},{7,5},{8,10},{9,7},{10,... | collective-permute-start | bytes 3538952 | tf_op jit(solution)/shard_map/ppermute | solution.py:62
  81.8 0.0 collective-permute-done.10.refs_15_.refs_16_
  81.8 0.0 collective-permute-start.15
  81.8 0.0 collective-permute-done.6.refs_2_
  81.8 0.0 copy-start.9
  81.8 3.2 %collective-permute-start.18 = (bf16[2,384,768]{2,1,0:T(8,128)(2,1)S(1)}, bf16[2,384,768]{2,1,0:T(8,128)(2,1)S(1)}, u32[]{:S(2)}, u32[]{:S(2)}) collective-permute-start(bf16[2,384,768]{2,1,0:T(8,128)(2,1)S(1)} %collective-permute-done.4.refs_10_.refs_11_), channel_id=1, source_target_pairs={{0,192},{1,49},{16,208},{17,1},{32,224},{33,17},{48,240},{49,33},{... | collective-permute-start | bytes 3538952 | tf_op jit(solution)/shard_map/ppermute | solution.py:63
  85.0 0.0 collective-permute-done.8.refs_16_.refs_17_
  85.0 0.0 copy-done.3
  85.0 0.1 collective-permute-start.9
  85.1 6.7 %collective-permute-done.17.refs_17_.refs_18_ = bf16[2,384,768]{2,1,0:T(8,128)(2,1)S(1)} collective-permute-done((bf16[2,384,768]{2,1,0:T(8,128)(2,1)S(1)}, bf16[2,384,768]{2,1,0:T(8,128)(2,1)S(1)}, u32[]{:S(2)}, u32[]{:S(2)}) %collective-permute-start.17) | collective-permute-done | bytes 1179680 | tf_op jit(solution)/shard_map/ppermute | solution.py:63
  91.8 1.3 collective-permute-start.19
  93.1 12.5 %collective-permute-done.14.refs_4_ = bf16[2,384,768]{2,1,0:T(8,128)(2,1)} collective-permute-done((bf16[2,384,768]{2,1,0:T(8,128)(2,1)S(1)}, bf16[2,384,768]{2,1,0:T(8,128)(2,1)}, u32[]{:S(2)}, u32[]{:S(2)}) %collective-permute-start.14) | collective-permute-done | bytes 1179680 | tf_op jit(solution)/shard_map/ppermute | solution.py:62
  105.6 2.7 %collective-permute-start.20 = (bf16[2,384,768]{2,1,0:T(8,128)(2,1)}, bf16[2,384,768]{2,1,0:T(8,128)(2,1)}, u32[]{:S(2)}, u32[]{:S(2)}) collective-permute-start(bf16[2,384,768]{2,1,0:T(8,128)(2,1)} %collective-permute-done.10.refs_15_.refs_16_), channel_id=1, source_target_pairs={{0,192},{1,49},{16,208},{17,1},{32,224},{33,17},{48,240},{49,33},{... | collective-permute-start | bytes 3538952 | tf_op jit(solution)/shard_map/ppermute | solution.py:63
  108.2 0.0 collective-permute-done.15.refs_18_.refs_19_
  108.2 3.8 %collective-permute-start.16 = (bf16[2,384,768]{2,1,0:T(8,128)(2,1)}, bf16[2,384,768]{2,1,0:T(8,128)(2,1)}, u32[]{:S(2)}, u32[]{:S(2)}) collective-permute-start(bf16[2,384,768]{2,1,0:T(8,128)(2,1)} %collective-permute-done.14.refs_4_), channel_id=1, source_target_pairs={{0,2},{1,15},{2,4},{3,1},{4,6},{5,3},{6,8},{7,5},{8,10},{9,7},{10,... | collective-permute-start | bytes 3538952 | tf_op jit(solution)/shard_map/ppermute | solution.py:62
  112.0 0.0 collective-permute-done.18.refs_19_.refs_20_
  112.0 0.0 copy-done.4
  112.0 0.1 collective-permute-start.21
  112.1 0.0 copy-done.5
  112.1 0.0 copy-done.6
  112.2 0.0 copy-done.7
  112.2 0.0 copy-done.8
  112.2 0.0 copy-done.9
  112.2 0.0 copy-done.10
  112.2 0.0 copy-done.11
  112.2 0.9 copy-done.12
  113.1 2.0 %collective-permute-done.9.refs_3_ = bf16[2,384,768]{2,1,0:T(8,128)(2,1)} collective-permute-done((bf16[2,384,768]{2,1,0:T(8,128)(2,1)S(1)}, bf16[2,384,768]{2,1,0:T(8,128)(2,1)}, u32[]{:S(2)}, u32[]{:S(2)}) %collective-permute-start.9) | collective-permute-done | bytes 1179680 | tf_op jit(solution)/shard_map/ppermute | solution.py:62
  115.1 0.0 copy-done
  115.1 0.0 copy-done.1
  115.1 0.0 copy-done.2
  115.1 19.8 %shard_map.17.refs_24_ = f32[2,384,768]{2,1,0:T(8,128)} custom-call(bf16[2,384,768]{2,1,0:T(8,128)(2,1)} %refs_8_.1, bf16[2,384,768]{2,1,0:T(8,128)(2,1)} %copy-done.5, bf16[2,384,768]{2,1,0:T(8,128)(2,1)} %copy-done.9, bf16[2,384,768]{2,1,0:T(8,128)(2,1)} %collective-permute-done.9.refs_3_, bf16[2,384,768]{2,1,0:T(8,128)(2,1)} %collective-permute-done.14.refs_4_, ...), custom_call_target="tpu_custom_call" | custom-call | flops 11777605632 | bytes 20971520 | tf_op jit(solution)/shard_map/pallas_call | solution.py:199
  135.0 0.0 collective-permute-done.19.refs_21_
  135.0 0.0 collective-permute-done.20.refs_22_
  135.0 0.0 collective-permute-done.16.refs_7_
  135.0 0.0 collective-permute-done.21.refs_23_
  135.0 10.3 %shard_map.18 = f32[2,384,768]{2,1,0:T(8,128)} custom-call(bf16[2,384,768]{2,1,0:T(8,128)(2,1)} %refs_8_.1, bf16[2,384,768]{2,1,0:T(8,128)(2,1)} %copy-done.5, bf16[2,384,768]{2,1,0:T(8,128)(2,1)} %copy-done.9, bf16[2,384,768]{2,1,0:T(8,128)(2,1)} %collective-permute-done.9.refs_3_, bf16[2,384,768]{2,1,0:T(8,128)(2,1)} %collective-permute-done.14.refs_4_, ...), custom_call_target="tpu_custom_call" | custom-call | flops 4529848320 | bytes 25165824 | tf_op jit(solution)/shard_map/pallas_call | solution.py:199
  (8 shorter events, 0.0 us)
Async XLA Ops:
  0.0 17.6 %collective-permute-start.1 = (bf16[2,384,768]{2,1,0:T(8,128)(2,1)}, bf16[2,384,768]{2,1,0:T(8,128)(2,1)S(1)}, u32[]{:S(2)}, u32[]{:S(2)}) collective-permute-start(bf16[2,384,768]{2,1,0:T(8,128)(2,1)} %refs_8_.1), channel_id=1, source_target_pairs={{0,16},{1,65},{16,32},{17,81},{32,48},{33,97},{48,0},{49,113},{64,... | collective-permute-start | bytes 3538952 | tf_op jit(solution)/shard_map/ppermute | solution.py:63
  1.5 19.5 %collective-permute-start = (bf16[2,384,768]{2,1,0:T(8,128)(2,1)}, bf16[2,384,768]{2,1,0:T(8,128)(2,1)S(1)}, u32[]{:S(2)}, u32[]{:S(2)}) collective-permute-start(bf16[2,384,768]{2,1,0:T(8,128)(2,1)} %refs_8_.1), channel_id=1, source_target_pairs={{0,48},{1,193},{16,0},{17,209},{32,16},{33,225},{48,32},{49,241},{... | collective-permute-start | bytes 3538952 | tf_op jit(solution)/shard_map/ppermute | solution.py:63
  3.2 17.8 %collective-permute-start.3 = (bf16[2,384,768]{2,1,0:T(8,128)(2,1)}, bf16[2,384,768]{2,1,0:T(8,128)(2,1)S(1)}, u32[]{:S(2)}, u32[]{:S(2)}) collective-permute-start(bf16[2,384,768]{2,1,0:T(8,128)(2,1)} %refs_8_.1), channel_id=1, source_target_pairs={{0,2},{1,15},{2,4},{3,1},{4,6},{5,3},{6,8},{7,5},{8,10},{9,7},{10,... | collective-permute-start | bytes 3538952 | tf_op jit(solution)/shard_map/ppermute | solution.py:62
  17.6 97.5 %copy-start = (bf16[2,384,768]{2,1,0:T(8,128)(2,1)}, bf16[2,384,768]{2,1,0:T(8,128)(2,1)S(1)}, u32[]{:S(2)}) copy-start(bf16[2,384,768]{2,1,0:T(8,128)(2,1)S(1)} %collective-permute-done.1.refs_8_.refs_9_) | copy-start | bytes 3538948
  17.6 26.3 %collective-permute-start.4 = (bf16[2,384,768]{2,1,0:T(8,128)(2,1)S(1)}, bf16[2,384,768]{2,1,0:T(8,128)(2,1)S(1)}, u32[]{:S(2)}, u32[]{:S(2)}) collective-permute-start(bf16[2,384,768]{2,1,0:T(8,128)(2,1)S(1)} %collective-permute-done.1.refs_8_.refs_9_), channel_id=1, source_target_pairs={{0,16},{1,65},{16,32},{17,81},{32,48},{33,97},{48,0},{49,113},{64,... | collective-permute-start | bytes 3538952 | tf_op jit(solution)/shard_map/ppermute | solution.py:63
  17.9 31.3 %collective-permute-start.11 = (bf16[2,384,768]{2,1,0:T(8,128)(2,1)}, bf16[2,384,768]{2,1,0:T(8,128)(2,1)S(1)}, u32[]{:S(2)}, u32[]{:S(2)}) collective-permute-start(bf16[2,384,768]{2,1,0:T(8,128)(2,1)} %refs_8_.1), channel_id=1, source_target_pairs={{0,192},{1,49},{16,208},{17,1},{32,224},{33,17},{48,240},{49,33},{... | collective-permute-start | bytes 3538952 | tf_op jit(solution)/shard_map/ppermute | solution.py:63
  20.9 29.9 %collective-permute-start.2 = (bf16[2,384,768]{2,1,0:T(8,128)(2,1)}, bf16[2,384,768]{2,1,0:T(8,128)(2,1)S(1)}, u32[]{:S(2)}, u32[]{:S(2)}) collective-permute-start(bf16[2,384,768]{2,1,0:T(8,128)(2,1)} %refs_8_.1), channel_id=1, source_target_pairs={{0,14},{1,3},{2,0},{3,5},{4,2},{5,7},{6,4},{7,9},{8,6},{9,11},{10,... | collective-permute-start | bytes 3538952 | tf_op jit(solution)/shard_map/ppermute | solution.py:62
  21.0 94.1 %copy-start.1 = (bf16[2,384,768]{2,1,0:T(8,128)(2,1)}, bf16[2,384,768]{2,1,0:T(8,128)(2,1)S(1)}, u32[]{:S(2)}) copy-start(bf16[2,384,768]{2,1,0:T(8,128)(2,1)S(1)} %collective-permute-done.refs_9_.refs_10_) | copy-start | bytes 3538948
  21.0 31.4 %collective-permute-start.5 = (bf16[2,384,768]{2,1,0:T(8,128)(2,1)}, bf16[2,384,768]{2,1,0:T(8,128)(2,1)S(1)}, u32[]{:S(2)}, u32[]{:S(2)}) collective-permute-start(bf16[2,384,768]{2,1,0:T(8,128)(2,1)} %refs_8_.1), channel_id=1, source_target_pairs={{0,64},{1,17},{16,80},{17,33},{32,96},{33,49},{48,112},{49,1},{64,... | collective-permute-start | bytes 3538952 | tf_op jit(solution)/shard_map/ppermute | solution.py:63
  21.1 94.1 %copy-start.2 = (bf16[2,384,768]{2,1,0:T(8,128)(2,1)}, bf16[2,384,768]{2,1,0:T(8,128)(2,1)S(1)}, u32[]{:S(2)}) copy-start(bf16[2,384,768]{2,1,0:T(8,128)(2,1)S(1)} %collective-permute-done.3.refs_6_) | copy-start | bytes 3538948
  21.1 31.4 %collective-permute-start.7 = (bf16[2,384,768]{2,1,0:T(8,128)(2,1)S(1)}, bf16[2,384,768]{2,1,0:T(8,128)(2,1)S(1)}, u32[]{:S(2)}, u32[]{:S(2)}) collective-permute-start(bf16[2,384,768]{2,1,0:T(8,128)(2,1)S(1)} %collective-permute-done.1.refs_8_.refs_9_), channel_id=1, source_target_pairs={{0,192},{1,49},{16,208},{17,1},{32,224},{33,17},{48,240},{49,33},{... | collective-permute-start | bytes 3538952 | tf_op jit(solution)/shard_map/ppermute | solution.py:63
  44.0 41.0 %copy-start.3 = (bf16[2,384,768]{2,1,0:T(8,128)(2,1)}, bf16[2,384,768]{2,1,0:T(8,128)(2,1)S(1)}, u32[]{:S(2)}) copy-start(bf16[2,384,768]{2,1,0:T(8,128)(2,1)S(1)} %collective-permute-done.4.refs_10_.refs_11_) | copy-start | bytes 3538948
  44.0 31.2 %collective-permute-start.12 = (bf16[2,384,768]{2,1,0:T(8,128)(2,1)S(1)}, bf16[2,384,768]{2,1,0:T(8,128)(2,1)S(1)}, u32[]{:S(2)}, u32[]{:S(2)}) collective-permute-start(bf16[2,384,768]{2,1,0:T(8,128)(2,1)S(1)} %collective-permute-done.3.refs_6_), channel_id=1, source_target_pairs={{0,2},{1,15},{2,4},{3,1},{4,6},{5,3},{6,8},{7,5},{8,10},{9,7},{10,... | collective-permute-start | bytes 3538952 | tf_op jit(solution)/shard_map/ppermute | solution.py:62
  49.2 62.8 %copy-start.4 = (bf16[2,384,768]{2,1,0:T(8,128)(2,1)}, bf16[2,384,768]{2,1,0:T(8,128)(2,1)S(1)}, u32[]{:S(2)}) copy-start(bf16[2,384,768]{2,1,0:T(8,128)(2,1)S(1)} %collective-permute-done.11.refs_11_.refs_12_) | copy-start | bytes 3538948
  49.2 28.9 %collective-permute-start.13 = (bf16[2,384,768]{2,1,0:T(8,128)(2,1)S(1)}, bf16[2,384,768]{2,1,0:T(8,128)(2,1)}, u32[]{:S(2)}, u32[]{:S(2)}) collective-permute-start(bf16[2,384,768]{2,1,0:T(8,128)(2,1)S(1)} %collective-permute-done.1.refs_8_.refs_9_), channel_id=1, source_target_pairs={{0,64},{1,17},{16,80},{17,33},{32,96},{33,49},{48,112},{49,1},{64,... | collective-permute-start | bytes 3538952 | tf_op jit(solution)/shard_map/ppermute | solution.py:63
  50.8 61.3 %copy-start.5 = (bf16[2,384,768]{2,1,0:T(8,128)(2,1)}, bf16[2,384,768]{2,1,0:T(8,128)(2,1)S(1)}, u32[]{:S(2)}) copy-start(bf16[2,384,768]{2,1,0:T(8,128)(2,1)S(1)} %collective-permute-done.2.refs_1_) | copy-start | bytes 3538948
  50.8 31.0 %collective-permute-start.10 = (bf16[2,384,768]{2,1,0:T(8,128)(2,1)S(1)}, bf16[2,384,768]{2,1,0:T(8,128)(2,1)}, u32[]{:S(2)}, u32[]{:S(2)}) collective-permute-start(bf16[2,384,768]{2,1,0:T(8,128)(2,1)S(1)} %collective-permute-done.refs_9_.refs_10_), channel_id=1, source_target_pairs={{0,192},{1,49},{16,208},{17,1},{32,224},{33,17},{48,240},{49,33},{... | collective-permute-start | bytes 3538952 | tf_op jit(solution)/shard_map/ppermute | solution.py:63
  52.5 59.7 %copy-start.6 = (bf16[2,384,768]{2,1,0:T(8,128)(2,1)}, bf16[2,384,768]{2,1,0:T(8,128)(2,1)S(1)}, u32[]{:S(2)}) copy-start(bf16[2,384,768]{2,1,0:T(8,128)(2,1)S(1)} %collective-permute-done.5.refs_12_.refs_13_) | copy-start | bytes 3538948
  52.5 29.3 %collective-permute-start.6 = (bf16[2,384,768]{2,1,0:T(8,128)(2,1)S(1)}, bf16[2,384,768]{2,1,0:T(8,128)(2,1)S(1)}, u32[]{:S(2)}, u32[]{:S(2)}) collective-permute-start(bf16[2,384,768]{2,1,0:T(8,128)(2,1)S(1)} %collective-permute-done.2.refs_1_), channel_id=1, source_target_pairs={{0,14},{1,3},{2,0},{3,5},{4,2},{5,7},{6,4},{7,9},{8,6},{9,11},{10,... | collective-permute-start | bytes 3538952 | tf_op jit(solution)/shard_map/ppermute | solution.py:62
  52.5 59.7 %copy-start.7 = (bf16[2,384,768]{2,1,0:T(8,128)(2,1)}, bf16[2,384,768]{2,1,0:T(8,128)(2,1)S(1)}, u32[]{:S(2)}) copy-start(bf16[2,384,768]{2,1,0:T(8,128)(2,1)S(1)} %collective-permute-done.7.refs_13_.refs_14_) | copy-start | bytes 3538948
  52.5 32.5 %collective-permute-start.8 = (bf16[2,384,768]{2,1,0:T(8,128)(2,1)S(1)}, bf16[2,384,768]{2,1,0:T(8,128)(2,1)S(1)}, u32[]{:S(2)}, u32[]{:S(2)}) collective-permute-start(bf16[2,384,768]{2,1,0:T(8,128)(2,1)S(1)} %collective-permute-done.refs_9_.refs_10_), channel_id=1, source_target_pairs={{0,64},{1,17},{16,80},{17,33},{32,96},{33,49},{48,112},{49,1},{64,... | collective-permute-start | bytes 3538952 | tf_op jit(solution)/shard_map/ppermute | solution.py:63
  75.2 37.0 %copy-start.8 = (bf16[2,384,768]{2,1,0:T(8,128)(2,1)}, bf16[2,384,768]{2,1,0:T(8,128)(2,1)S(1)}, u32[]{:S(2)}) copy-start(bf16[2,384,768]{2,1,0:T(8,128)(2,1)S(1)} %collective-permute-done.12.refs_5_) | copy-start | bytes 3538948
  75.2 16.6 %collective-permute-start.17 = (bf16[2,384,768]{2,1,0:T(8,128)(2,1)S(1)}, bf16[2,384,768]{2,1,0:T(8,128)(2,1)S(1)}, u32[]{:S(2)}, u32[]{:S(2)}) collective-permute-start(bf16[2,384,768]{2,1,0:T(8,128)(2,1)S(1)} %collective-permute-done.11.refs_11_.refs_12_), channel_id=1, source_target_pairs={{0,192},{1,49},{16,208},{17,1},{32,224},{33,17},{48,240},{49,33},{... | collective-permute-start | bytes 3538952 | tf_op jit(solution)/shard_map/ppermute | solution.py:63
  78.1 27.5 %collective-permute-start.14 = (bf16[2,384,768]{2,1,0:T(8,128)(2,1)S(1)}, bf16[2,384,768]{2,1,0:T(8,128)(2,1)}, u32[]{:S(2)}, u32[]{:S(2)}) collective-permute-start(bf16[2,384,768]{2,1,0:T(8,128)(2,1)S(1)} %collective-permute-done.12.refs_5_), channel_id=1, source_target_pairs={{0,2},{1,15},{2,4},{3,1},{4,6},{5,3},{6,8},{7,5},{8,10},{9,7},{10,... | collective-permute-start | bytes 3538952 | tf_op jit(solution)/shard_map/ppermute | solution.py:62
  81.8 26.5 %collective-permute-start.15 = (bf16[2,384,768]{2,1,0:T(8,128)(2,1)S(1)}, bf16[2,384,768]{2,1,0:T(8,128)(2,1)}, u32[]{:S(2)}, u32[]{:S(2)}) collective-permute-start(bf16[2,384,768]{2,1,0:T(8,128)(2,1)S(1)} %collective-permute-done.4.refs_10_.refs_11_), channel_id=1, source_target_pairs={{0,64},{1,17},{16,80},{17,33},{32,96},{33,49},{48,112},{49,1},{64,... | collective-permute-start | bytes 3538952 | tf_op jit(solution)/shard_map/ppermute | solution.py:63
  81.8 30.4 %copy-start.9 = (bf16[2,384,768]{2,1,0:T(8,128)(2,1)}, bf16[2,384,768]{2,1,0:T(8,128)(2,1)S(1)}, u32[]{:S(2)}) copy-start(bf16[2,384,768]{2,1,0:T(8,128)(2,1)S(1)} %collective-permute-done.6.refs_2_) | copy-start | bytes 3538948
  81.8 30.3 %collective-permute-start.18 = (bf16[2,384,768]{2,1,0:T(8,128)(2,1)S(1)}, bf16[2,384,768]{2,1,0:T(8,128)(2,1)S(1)}, u32[]{:S(2)}, u32[]{:S(2)}) collective-permute-start(bf16[2,384,768]{2,1,0:T(8,128)(2,1)S(1)} %collective-permute-done.4.refs_10_.refs_11_), channel_id=1, source_target_pairs={{0,192},{1,49},{16,208},{17,1},{32,224},{33,17},{48,240},{49,33},{... | collective-permute-start | bytes 3538952 | tf_op jit(solution)/shard_map/ppermute | solution.py:63
  85.0 27.2 %copy-start.10 = (bf16[2,384,768]{2,1,0:T(8,128)(2,1)}, bf16[2,384,768]{2,1,0:T(8,128)(2,1)S(1)}, u32[]{:S(2)}) copy-start(bf16[2,384,768]{2,1,0:T(8,128)(2,1)S(1)} %collective-permute-done.8.refs_16_.refs_17_) | copy-start | bytes 3538948
  85.0 30.1 %collective-permute-start.9 = (bf16[2,384,768]{2,1,0:T(8,128)(2,1)S(1)}, bf16[2,384,768]{2,1,0:T(8,128)(2,1)}, u32[]{:S(2)}, u32[]{:S(2)}) collective-permute-start(bf16[2,384,768]{2,1,0:T(8,128)(2,1)S(1)} %collective-permute-done.6.refs_2_), channel_id=1, source_target_pairs={{0,14},{1,3},{2,0},{3,5},{4,2},{5,7},{6,4},{7,9},{8,6},{9,11},{10,... | collective-permute-start | bytes 3538952 | tf_op jit(solution)/shard_map/ppermute | solution.py:62
  91.8 20.4 %copy-start.11 = (bf16[2,384,768]{2,1,0:T(8,128)(2,1)}, bf16[2,384,768]{2,1,0:T(8,128)(2,1)S(1)}, u32[]{:S(2)}) copy-start(bf16[2,384,768]{2,1,0:T(8,128)(2,1)S(1)} %collective-permute-done.17.refs_17_.refs_18_) | copy-start | bytes 3538948
  91.8 43.2 %collective-permute-start.19 = (bf16[2,384,768]{2,1,0:T(8,128)(2,1)}, bf16[2,384,768]{2,1,0:T(8,128)(2,1)}, u32[]{:S(2)}, u32[]{:S(2)}) collective-permute-start(bf16[2,384,768]{2,1,0:T(8,128)(2,1)} %collective-permute-done.13.refs_14_.refs_15_), channel_id=1, source_target_pairs={{0,64},{1,17},{16,80},{17,33},{32,96},{33,49},{48,112},{49,1},{64,... | collective-permute-start | bytes 3538952 | tf_op jit(solution)/shard_map/ppermute | solution.py:63
  105.6 29.4 %collective-permute-start.20 = (bf16[2,384,768]{2,1,0:T(8,128)(2,1)}, bf16[2,384,768]{2,1,0:T(8,128)(2,1)}, u32[]{:S(2)}, u32[]{:S(2)}) collective-permute-start(bf16[2,384,768]{2,1,0:T(8,128)(2,1)} %collective-permute-done.10.refs_15_.refs_16_), channel_id=1, source_target_pairs={{0,192},{1,49},{16,208},{17,1},{32,224},{33,17},{48,240},{49,33},{... | collective-permute-start | bytes 3538952 | tf_op jit(solution)/shard_map/ppermute | solution.py:63
  108.2 26.7 %collective-permute-start.16 = (bf16[2,384,768]{2,1,0:T(8,128)(2,1)}, bf16[2,384,768]{2,1,0:T(8,128)(2,1)}, u32[]{:S(2)}, u32[]{:S(2)}) collective-permute-start(bf16[2,384,768]{2,1,0:T(8,128)(2,1)} %collective-permute-done.14.refs_4_), channel_id=1, source_target_pairs={{0,2},{1,15},{2,4},{3,1},{4,6},{5,3},{6,8},{7,5},{8,10},{9,7},{10,... | collective-permute-start | bytes 3538952 | tf_op jit(solution)/shard_map/ppermute | solution.py:62
  112.0 1.1 copy-start.12
  112.0 22.9 %collective-permute-start.21 = (bf16[2,384,768]{2,1,0:T(8,128)(2,1)}, bf16[2,384,768]{2,1,0:T(8,128)(2,1)}, u32[]{:S(2)}, u32[]{:S(2)}) collective-permute-start(bf16[2,384,768]{2,1,0:T(8,128)(2,1)} %collective-permute-done.15.refs_18_.refs_19_), channel_id=1, source_target_pairs={{0,64},{1,17},{16,80},{17,33},{32,96},{33,49},{48,112},{49,1},{64,... | collective-permute-start | bytes 3538952 | tf_op jit(solution)/shard_map/ppermute | solution.py:63

commit v3 on v2

--- a/solution.py
+++ b/solution.py
@@ -9,6 +9,7 @@
 
 NS = 6144
 WINDOW = 5
+COLUMNS = 256
 
 
 def plane_pairs(first, hop):
@@ -147,16 +148,15 @@
     keys = NEAR + (4,)
     lefts = [refs.pop(0) for _ in keys]
     rights = [refs.pop(0) for _ in EARLY + LATE]
-    total, out, l_buf, r_buf, sems, flags = refs
+    total, out, l_buf, r_buf, sems, flags, acc = refs
     here = lax.axis_index("src")
     depth = l_buf.shape[-1]
     tasks = []
+    for part in range(2):
+        owner = 2 * ((here + 4) % 8) + part
+        tasks.append((owner, key_code(owner)))
     for key in LATE:
         tasks.append((owner_of(key), None))
-    for part in range(2):
-        owner = 2 * ((here + 4) % 8) + part
-        code = key_code(owner)
-        tasks.append((owner, code))
 
     def is_early(code):
         hit = code == 0
@@ -166,7 +166,7 @@
 
     for k, (owner, code) in enumerate(tasks):
         if code is None:
-            pltpu.make_async_copy(rights[len(EARLY) + k], r_buf.at[k], sems.at[k, 0]).start()
+            pltpu.make_async_copy(rights[len(EARLY) + k - 2], r_buf.at[k], sems.at[k, 0]).start()
             pick_left(owner, lefts, keys, l_buf.at[k], sems.at[k, 1])
         else:
             for ref, (a, b) in zip(rights, EARLY):
@@ -178,7 +178,7 @@
 
     for k, (_, code) in enumerate(tasks):
         flags[k] = 1 if code is None else is_early(code).astype(jnp.int32)
-    out[...] = total[...]
+    acc[...] = total[...]
 
     def step(k, carry):
         pltpu.make_async_copy(lefts[0].at[:, :, pl.ds(0, depth)], l_buf.at[k], sems.at[k, 1]).wait()
@@ -186,26 +186,37 @@
         @pl.when(flags[k] == 1)
         def _():
             pltpu.make_async_copy(rights[0], r_buf.at[k], sems.at[k, 0]).wait()
-            out[...] += product(l_buf[k], r_buf[k])
+            acc[...] += product(l_buf[k], r_buf[k])
 
         return carry
 
-    lax.fori_loop(0, len(tasks), step, 0)
-    out[...] *= scale
-
-
-def call(kernel, operands, n_outside, slots, flops, depth, width, dtype):
+    last = len(tasks) - 1
+    lax.fori_loop(0, last, step, 0)
+    pltpu.make_async_copy(lefts[0].at[:, :, pl.ds(0, depth)], l_buf.at[last], sems.at[last, 1]).wait()
+    pltpu.make_async_copy(rights[0], r_buf.at[last], sems.at[last, 0]).wait()
+    copies = []
+    for k in range(3):
+        tile = pl.ds(k * COLUMNS, COLUMNS)
+        acc[:, :, tile] = (acc[:, :, tile] + product(l_buf[last], r_buf[last, :, :, tile])) * scale
+        copies.append(pltpu.make_async_copy(acc.at[:, :, tile], out.at[:, :, tile], sems.at[k, 0]))
+        copies[-1].start()
+    for copy in copies:
+        copy.wait()
+
+
+def call(kernel, operands, n_outside, slots, flops, depth, width, dtype, extra=()):
     inside, outside = pl.BlockSpec(memory_space=pltpu.VMEM), pl.BlockSpec(memory_space=pl.ANY)
     return pl.pallas_call(
         kernel,
         out_shape=jax.ShapeDtypeStruct((2, depth, width), jnp.float32),
         in_specs=[outside] * n_outside + [inside] * (len(operands) - n_outside),
-        out_specs=inside,
+        out_specs=outside if extra else inside,
         scratch_shapes=[
             pltpu.VMEM((slots, 2, depth, depth), dtype),
             pltpu.VMEM((slots, 2, depth, width), dtype),
             pltpu.SemaphoreType.DMA((slots, 2)),
             pltpu.SMEM((16,), jnp.int32),
+            *extra,
         ],
         compiler_params=pltpu.CompilerParams(vmem_limit_bytes=60 * 2**20),
         cost_estimate=pl.CostEstimate(flops=flops, bytes_accessed=n_outside * 2**20, transcendentals=0),
@@ -229,7 +240,7 @@
     total = call(early_kernel, early, len(early), 2, unit * len(EARLY), depth, width, dtype)
     late = [held[key] for key in list(NEAR) + [4] + EARLY + LATE]
     kernel = functools.partial(late_kernel, 1.0 / float(NS) ** 0.5)
-    return call(kernel, late + [total], len(late), len(LATE) + 2, unit * (len(LATE) + 2), depth, width, dtype)
+    return call(kernel, late + [total], len(late), len(LATE) + 2, unit * (len(LATE) + 2), depth, width, dtype, [pltpu.VMEM((2, depth, width), jnp.float32)])
 
 
 def solution(mesh):

time: 146 us -> 145 us (level)
  no operation moved by 1% of the time
where the time goes in v3:
time: 145 us
  waiting for transfers between devices  74.4 us (51%)
  starting transfers between devices  39.6 us (27%)
  Pallas kernels  29.7 us (20%)
    ppermute x15, waiting for transfers between devices, move(): return lax.ppermute(value, ('rcv', 'freq'), plane_pairs(axis == 'a', hop))  37.7 us
    ppermute x7, waiting for transfers between devices, move(): return lax.ppermute(value, ('src', 'freq'), ring_pairs(hop))  36.8 us
    pallas_call x2, Pallas kernels, call(): pl.pallas_call(kernel, out_shape=jax.ShapeDtypeStruct((2, depth, width),...  29.7 us
    ppermute x15, starting transfers between devices, move(): return lax.ppermute(value, ('rcv', 'freq'), plane_pairs(axis == 'a', hop))  23.6 us
    ppermute x7, starting transfers between devices, move(): return lax.ppermute(value, ('src', 'freq'), ring_pairs(hop))  16 us
  transfers between devices with their start and end apart: 22, of which 6 were waited for; matrix products, arithmetic and copies ran while one was open for 0% of the time, Pallas kernels for 14%

profile of v3, /device:TPU:96, one launch (start us, length us, event | category | flops | bytes accessed | tf_op | source)
XLA Modules:
  0.0 145.0 jit_solution(1601622429295807303)
XLA Ops:
  0.0 1.5 %collective-permute-start.1 = (bf16[2,384,768]{2,1,0:T(8,128)(2,1)}, bf16[2,384,768]{2,1,0:T(8,128)(2,1)S(1)}, u32[]{:S(2)}, u32[]{:S(2)}) collective-permute-start(bf16[2,384,768]{2,1,0:T(8,128)(2,1)} %refs_8_.1), channel_id=1, source_target_pairs={{0,16},{1,65},{16,32},{17,81},{32,48},{33,97},{48,0},{49,113},{64,... | collective-permute-start | bytes 3538952 | tf_op jit(solution)/shard_map/ppermute | solution.py:64
  1.5 1.7 %collective-permute-start = (bf16[2,384,768]{2,1,0:T(8,128)(2,1)}, bf16[2,384,768]{2,1,0:T(8,128)(2,1)S(1)}, u32[]{:S(2)}, u32[]{:S(2)}) collective-permute-start(bf16[2,384,768]{2,1,0:T(8,128)(2,1)} %refs_8_.1), channel_id=1, source_target_pairs={{0,48},{1,193},{16,0},{17,209},{32,16},{33,225},{48,32},{49,241},{... | collective-permute-start | bytes 3538952 | tf_op jit(solution)/shard_map/ppermute | solution.py:64
  3.2 3.1 %collective-permute-start.3 = (bf16[2,384,768]{2,1,0:T(8,128)(2,1)}, bf16[2,384,768]{2,1,0:T(8,128)(2,1)S(1)}, u32[]{:S(2)}, u32[]{:S(2)}) collective-permute-start(bf16[2,384,768]{2,1,0:T(8,128)(2,1)} %refs_8_.1), channel_id=1, source_target_pairs={{0,2},{1,15},{2,4},{3,1},{4,6},{5,3},{6,8},{7,5},{8,10},{9,7},{10,... | collective-permute-start | bytes 3538952 | tf_op jit(solution)/shard_map/ppermute | solution.py:63
  6.4 11.3 %collective-permute-done.1.refs_8_.refs_9_ = bf16[2,384,768]{2,1,0:T(8,128)(2,1)S(1)} collective-permute-done((bf16[2,384,768]{2,1,0:T(8,128)(2,1)}, bf16[2,384,768]{2,1,0:T(8,128)(2,1)S(1)}, u32[]{:S(2)}, u32[]{:S(2)}) %collective-permute-start.1) | collective-permute-done | bytes 1179680 | tf_op jit(solution)/shard_map/ppermute | solution.py:64
  17.6 0.0 copy-start
  17.6 0.3 collective-permute-start.4
  17.9 3.0 %collective-permute-start.11 = (bf16[2,384,768]{2,1,0:T(8,128)(2,1)}, bf16[2,384,768]{2,1,0:T(8,128)(2,1)S(1)}, u32[]{:S(2)}, u32[]{:S(2)}) collective-permute-start(bf16[2,384,768]{2,1,0:T(8,128)(2,1)} %refs_8_.1), channel_id=1, source_target_pairs={{0,192},{1,49},{16,208},{17,1},{32,224},{33,17},{48,240},{49,33},{... | collective-permute-start | bytes 3538952 | tf_op jit(solution)/shard_map/ppermute | solution.py:64
  20.9 0.1 collective-permute-start.2
  21.0 0.0 collective-permute-done.refs_9_.refs_10_
  21.0 0.0 copy-start.1
  21.0 0.0 collective-permute-start.5
  21.0 0.0 collective-permute-done.3.refs_6_
  21.1 0.0 copy-start.2
  21.1 3.2 %collective-permute-start.7 = (bf16[2,384,768]{2,1,0:T(8,128)(2,1)S(1)}, bf16[2,384,768]{2,1,0:T(8,128)(2,1)S(1)}, u32[]{:S(2)}, u32[]{:S(2)}) collective-permute-start(bf16[2,384,768]{2,1,0:T(8,128)(2,1)S(1)} %collective-permute-done.1.refs_8_.refs_9_), channel_id=1, source_target_pairs={{0,192},{1,49},{16,208},{17,1},{32,224},{33,17},{48,240},{49,33},{... | collective-permute-start | bytes 3538952 | tf_op jit(solution)/shard_map/ppermute | solution.py:64
  24.3 19.7 %collective-permute-done.4.refs_10_.refs_11_ = bf16[2,384,768]{2,1,0:T(8,128)(2,1)S(1)} collective-permute-done((bf16[2,384,768]{2,1,0:T(8,128)(2,1)S(1)}, bf16[2,384,768]{2,1,0:T(8,128)(2,1)S(1)}, u32[]{:S(2)}, u32[]{:S(2)}) %collective-permute-start.4) | collective-permute-done | bytes 1179680 | tf_op jit(solution)/shard_map/ppermute | solution.py:64
  44.0 5.2 %collective-permute-start.12 = (bf16[2,384,768]{2,1,0:T(8,128)(2,1)S(1)}, bf16[2,384,768]{2,1,0:T(8,128)(2,1)S(1)}, u32[]{:S(2)}, u32[]{:S(2)}) collective-permute-start(bf16[2,384,768]{2,1,0:T(8,128)(2,1)S(1)} %collective-permute-done.3.refs_6_), channel_id=1, source_target_pairs={{0,2},{1,15},{2,4},{3,1},{4,6},{5,3},{6,8},{7,5},{8,10},{9,7},{10,... | collective-permute-start | bytes 3538952 | tf_op jit(solution)/shard_map/ppermute | solution.py:63
  49.2 0.0 collective-permute-done.11.refs_11_.refs_12_
  49.2 1.6 %collective-permute-start.13 = (bf16[2,384,768]{2,1,0:T(8,128)(2,1)S(1)}, bf16[2,384,768]{2,1,0:T(8,128)(2,1)}, u32[]{:S(2)}, u32[]{:S(2)}) collective-permute-start(bf16[2,384,768]{2,1,0:T(8,128)(2,1)S(1)} %collective-permute-done.1.refs_8_.refs_9_), channel_id=1, source_target_pairs={{0,64},{1,17},{16,80},{17,33},{32,96},{33,49},{48,112},{49,1},{64,... | collective-permute-start | bytes 3538952 | tf_op jit(solution)/shard_map/ppermute | solution.py:64
  50.8 0.0 collective-permute-done.2.refs_1_
  50.8 1.7 %collective-permute-start.10 = (bf16[2,384,768]{2,1,0:T(8,128)(2,1)S(1)}, bf16[2,384,768]{2,1,0:T(8,128)(2,1)}, u32[]{:S(2)}, u32[]{:S(2)}) collective-permute-start(bf16[2,384,768]{2,1,0:T(8,128)(2,1)S(1)} %collective-permute-done.refs_9_.refs_10_), channel_id=1, source_target_pairs={{0,192},{1,49},{16,208},{17,1},{32,224},{33,17},{48,240},{49,33},{... | collective-permute-start | bytes 3538952 | tf_op jit(solution)/shard_map/ppermute | solution.py:64
  52.5 0.0 collective-permute-done.5.refs_12_.refs_13_
  52.5 0.0 collective-permute-start.6
  52.5 0.0 collective-permute-done.7.refs_13_.refs_14_
  52.5 0.0 copy-start.7
  52.5 0.4 collective-permute-start.8
  52.9 22.3 %collective-permute-done.12.refs_5_ = bf16[2,384,768]{2,1,0:T(8,128)(2,1)S(1)} collective-permute-done((bf16[2,384,768]{2,1,0:T(8,128)(2,1)S(1)}, bf16[2,384,768]{2,1,0:T(8,128)(2,1)S(1)}, u32[]{:S(2)}, u32[]{:S(2)}) %collective-permute-start.12) | collective-permute-done | bytes 1179680 | tf_op jit(solution)/shard_map/ppermute | solution.py:63
  75.2 2.9 %collective-permute-start.17 = (bf16[2,384,768]{2,1,0:T(8,128)(2,1)S(1)}, bf16[2,384,768]{2,1,0:T(8,128)(2,1)S(1)}, u32[]{:S(2)}, u32[]{:S(2)}) collective-permute-start(bf16[2,384,768]{2,1,0:T(8,128)(2,1)S(1)} %collective-permute-done.11.refs_11_.refs_12_), channel_id=1, source_target_pairs={{0,192},{1,49},{16,208},{17,1},{32,224},{33,17},{48,240},{49,33},{... | collective-permute-start | bytes 3538952 | tf_op jit(solution)/shard_map/ppermute | solution.py:64
  78.1 0.0 collective-permute-done.13.refs_14_.refs_15_
  78.1 3.7 %collective-permute-start.14 = (bf16[2,384,768]{2,1,0:T(8,128)(2,1)S(1)}, bf16[2,384,768]{2,1,0:T(8,128)(2,1)}, u32[]{:S(2)}, u32[]{:S(2)}) collective-permute-start(bf16[2,384,768]{2,1,0:T(8,128)(2,1)S(1)} %collective-permute-done.12.refs_5_), channel_id=1, source_target_pairs={{0,2},{1,15},{2,4},{3,1},{4,6},{5,3},{6,8},{7,5},{8,10},{9,7},{10,... | collective-permute-start | bytes 3538952 | tf_op jit(solution)/shard_map/ppermute | solution.py:63
  81.8 0.0 collective-permute-done.10.refs_15_.refs_16_
  81.8 0.0 collective-permute-start.15
  81.8 0.0 collective-permute-done.6.refs_2_
  81.8 0.0 copy-start.9
  81.8 3.2 %collective-permute-start.18 = (bf16[2,384,768]{2,1,0:T(8,128)(2,1)S(1)}, bf16[2,384,768]{2,1,0:T(8,128)(2,1)S(1)}, u32[]{:S(2)}, u32[]{:S(2)}) collective-permute-start(bf16[2,384,768]{2,1,0:T(8,128)(2,1)S(1)} %collective-permute-done.4.refs_10_.refs_11_), channel_id=1, source_target_pairs={{0,192},{1,49},{16,208},{17,1},{32,224},{33,17},{48,240},{49,33},{... | collective-permute-start | bytes 3538952 | tf_op jit(solution)/shard_map/ppermute | solution.py:64
  85.0 0.0 collective-permute-done.8.refs_16_.refs_17_
  85.0 0.0 copy-done.3
  85.0 0.1 collective-permute-start.9
  85.1 6.7 %collective-permute-done.17.refs_17_.refs_18_ = bf16[2,384,768]{2,1,0:T(8,128)(2,1)S(1)} collective-permute-done((bf16[2,384,768]{2,1,0:T(8,128)(2,1)S(1)}, bf16[2,384,768]{2,1,0:T(8,128)(2,1)S(1)}, u32[]{:S(2)}, u32[]{:S(2)}) %collective-permute-start.17) | collective-permute-done | bytes 1179680 | tf_op jit(solution)/shard_map/ppermute | solution.py:64
  91.8 1.3 collective-permute-start.19
  93.1 12.5 %collective-permute-done.14.refs_4_ = bf16[2,384,768]{2,1,0:T(8,128)(2,1)} collective-permute-done((bf16[2,384,768]{2,1,0:T(8,128)(2,1)S(1)}, bf16[2,384,768]{2,1,0:T(8,128)(2,1)}, u32[]{:S(2)}, u32[]{:S(2)}) %collective-permute-start.14) | collective-permute-done | bytes 1179680 | tf_op jit(solution)/shard_map/ppermute | solution.py:63
  105.6 2.7 %collective-permute-start.20 = (bf16[2,384,768]{2,1,0:T(8,128)(2,1)}, bf16[2,384,768]{2,1,0:T(8,128)(2,1)}, u32[]{:S(2)}, u32[]{:S(2)}) collective-permute-start(bf16[2,384,768]{2,1,0:T(8,128)(2,1)} %collective-permute-done.10.refs_15_.refs_16_), channel_id=1, source_target_pairs={{0,192},{1,49},{16,208},{17,1},{32,224},{33,17},{48,240},{49,33},{... | collective-permute-start | bytes 3538952 | tf_op jit(solution)/shard_map/ppermute | solution.py:64
  108.2 0.0 collective-permute-done.15.refs_18_.refs_19_
  108.2 3.8 %collective-permute-start.16 = (bf16[2,384,768]{2,1,0:T(8,128)(2,1)}, bf16[2,384,768]{2,1,0:T(8,128)(2,1)}, u32[]{:S(2)}, u32[]{:S(2)}) collective-permute-start(bf16[2,384,768]{2,1,0:T(8,128)(2,1)} %collective-permute-done.14.refs_4_), channel_id=1, source_target_pairs={{0,2},{1,15},{2,4},{3,1},{4,6},{5,3},{6,8},{7,5},{8,10},{9,7},{10,... | collective-permute-start | bytes 3538952 | tf_op jit(solution)/shard_map/ppermute | solution.py:63
  112.0 0.0 collective-permute-done.18.refs_19_.refs_20_
  112.0 0.0 copy-done.4
  112.0 0.1 collective-permute-start.21
  112.1 0.0 copy-done.5
  112.1 0.0 copy-done.6
  112.2 0.0 copy-done.7
  112.2 0.0 copy-done.8
  112.2 0.0 copy-done.9
  112.2 0.0 copy-done.10
  112.2 0.0 copy-done.11
  112.2 0.9 copy-done.12
  113.1 2.0 %collective-permute-done.9.refs_3_ = bf16[2,384,768]{2,1,0:T(8,128)(2,1)} collective-permute-done((bf16[2,384,768]{2,1,0:T(8,128)(2,1)S(1)}, bf16[2,384,768]{2,1,0:T(8,128)(2,1)}, u32[]{:S(2)}, u32[]{:S(2)}) %collective-permute-start.9) | collective-permute-done | bytes 1179680 | tf_op jit(solution)/shard_map/ppermute | solution.py:63
  115.1 0.0 copy-done
  115.1 0.0 copy-done.1
  115.1 0.0 copy-done.2
  115.1 19.8 %shard_map.17.refs_24_ = f32[2,384,768]{2,1,0:T(8,128)} custom-call(bf16[2,384,768]{2,1,0:T(8,128)(2,1)} %refs_8_.1, bf16[2,384,768]{2,1,0:T(8,128)(2,1)} %copy-done.5, bf16[2,384,768]{2,1,0:T(8,128)(2,1)} %copy-done.9, bf16[2,384,768]{2,1,0:T(8,128)(2,1)} %collective-permute-done.9.refs_3_, bf16[2,384,768]{2,1,0:T(8,128)(2,1)} %collective-permute-done.14.refs_4_, ...), custom_call_target="tpu_custom_call" | custom-call | flops 11777605632 | bytes 20971520 | tf_op jit(solution)/shard_map/pallas_call | solution.py:209
  135.0 0.0 collective-permute-done.19.refs_21_
  135.0 0.0 collective-permute-done.20.refs_22_
  135.0 0.0 collective-permute-done.16.refs_7_
  135.0 0.0 collective-permute-done.21.refs_23_
  135.0 9.8 %shard_map.18 = f32[2,384,768]{2,1,0:T(8,128)} custom-call(bf16[2,384,768]{2,1,0:T(8,128)(2,1)} %refs_8_.1, bf16[2,384,768]{2,1,0:T(8,128)(2,1)} %copy-done.5, bf16[2,384,768]{2,1,0:T(8,128)(2,1)} %copy-done.9, bf16[2,384,768]{2,1,0:T(8,128)(2,1)} %collective-permute-done.9.refs_3_, bf16[2,384,768]{2,1,0:T(8,128)(2,1)} %collective-permute-done.14.refs_4_, ...), custom_call_target="tpu_custom_call" | custom-call | flops 4529848320 | bytes 25165824 | tf_op jit(solution)/shard_map/pallas_call | solution.py:209
  (8 shorter events, 0.0 us)
Async XLA Ops:
  0.0 17.6 %collective-permute-start.1 = (bf16[2,384,768]{2,1,0:T(8,128)(2,1)}, bf16[2,384,768]{2,1,0:T(8,128)(2,1)S(1)}, u32[]{:S(2)}, u32[]{:S(2)}) collective-permute-start(bf16[2,384,768]{2,1,0:T(8,128)(2,1)} %refs_8_.1), channel_id=1, source_target_pairs={{0,16},{1,65},{16,32},{17,81},{32,48},{33,97},{48,0},{49,113},{64,... | collective-permute-start | bytes 3538952 | tf_op jit(solution)/shard_map/ppermute | solution.py:64
  1.5 19.5 %collective-permute-start = (bf16[2,384,768]{2,1,0:T(8,128)(2,1)}, bf16[2,384,768]{2,1,0:T(8,128)(2,1)S(1)}, u32[]{:S(2)}, u32[]{:S(2)}) collective-permute-start(bf16[2,384,768]{2,1,0:T(8,128)(2,1)} %refs_8_.1), channel_id=1, source_target_pairs={{0,48},{1,193},{16,0},{17,209},{32,16},{33,225},{48,32},{49,241},{... | collective-permute-start | bytes 3538952 | tf_op jit(solution)/shard_map/ppermute | solution.py:64
  3.2 17.8 %collective-permute-start.3 = (bf16[2,384,768]{2,1,0:T(8,128)(2,1)}, bf16[2,384,768]{2,1,0:T(8,128)(2,1)S(1)}, u32[]{:S(2)}, u32[]{:S(2)}) collective-permute-start(bf16[2,384,768]{2,1,0:T(8,128)(2,1)} %refs_8_.1), channel_id=1, source_target_pairs={{0,2},{1,15},{2,4},{3,1},{4,6},{5,3},{6,8},{7,5},{8,10},{9,7},{10,... | collective-permute-start | bytes 3538952 | tf_op jit(solution)/shard_map/ppermute | solution.py:63
  17.6 97.5 %copy-start = (bf16[2,384,768]{2,1,0:T(8,128)(2,1)}, bf16[2,384,768]{2,1,0:T(8,128)(2,1)S(1)}, u32[]{:S(2)}) copy-start(bf16[2,384,768]{2,1,0:T(8,128)(2,1)S(1)} %collective-permute-done.1.refs_8_.refs_9_) | copy-start | bytes 3538948
  17.6 26.3 %collective-permute-start.4 = (bf16[2,384,768]{2,1,0:T(8,128)(2,1)S(1)}, bf16[2,384,768]{2,1,0:T(8,128)(2,1)S(1)}, u32[]{:S(2)}, u32[]{:S(2)}) collective-permute-start(bf16[2,384,768]{2,1,0:T(8,128)(2,1)S(1)} %collective-permute-done.1.refs_8_.refs_9_), channel_id=1, source_target_pairs={{0,16},{1,65},{16,32},{17,81},{32,48},{33,97},{48,0},{49,113},{64,... | collective-permute-start | bytes 3538952 | tf_op jit(solution)/shard_map/ppermute | solution.py:64
  17.9 31.3 %collective-permute-start.11 = (bf16[2,384,768]{2,1,0:T(8,128)(2,1)}, bf16[2,384,768]{2,1,0:T(8,128)(2,1)S(1)}, u32[]{:S(2)}, u32[]{:S(2)}) collective-permute-start(bf16[2,384,768]{2,1,0:T(8,128)(2,1)} %refs_8_.1), channel_id=1, source_target_pairs={{0,192},{1,49},{16,208},{17,1},{32,224},{33,17},{48,240},{49,33},{... | collective-permute-start | bytes 3538952 | tf_op jit(solution)/shard_map/ppermute | solution.py:64
  20.9 29.9 %collective-permute-start.2 = (bf16[2,384,768]{2,1,0:T(8,128)(2,1)}, bf16[2,384,768]{2,1,0:T(8,128)(2,1)S(1)}, u32[]{:S(2)}, u32[]{:S(2)}) collective-permute-start(bf16[2,384,768]{2,1,0:T(8,128)(2,1)} %refs_8_.1), channel_id=1, source_target_pairs={{0,14},{1,3},{2,0},{3,5},{4,2},{5,7},{6,4},{7,9},{8,6},{9,11},{10,... | collective-permute-start | bytes 3538952 | tf_op jit(solution)/shard_map/ppermute | solution.py:63
  21.0 94.1 %copy-start.1 = (bf16[2,384,768]{2,1,0:T(8,128)(2,1)}, bf16[2,384,768]{2,1,0:T(8,128)(2,1)S(1)}, u32[]{:S(2)}) copy-start(bf16[2,384,768]{2,1,0:T(8,128)(2,1)S(1)} %collective-permute-done.refs_9_.refs_10_) | copy-start | bytes 3538948
  21.0 31.4 %collective-permute-start.5 = (bf16[2,384,768]{2,1,0:T(8,128)(2,1)}, bf16[2,384,768]{2,1,0:T(8,128)(2,1)S(1)}, u32[]{:S(2)}, u32[]{:S(2)}) collective-permute-start(bf16[2,384,768]{2,1,0:T(8,128)(2,1)} %refs_8_.1), channel_id=1, source_target_pairs={{0,64},{1,17},{16,80},{17,33},{32,96},{33,49},{48,112},{49,1},{64,... | collective-permute-start | bytes 3538952 | tf_op jit(solution)/shard_map/ppermute | solution.py:64
  21.1 94.1 %copy-start.2 = (bf16[2,384,768]{2,1,0:T(8,128)(2,1)}, bf16[2,384,768]{2,1,0:T(8,128)(2,1)S(1)}, u32[]{:S(2)}) copy-start(bf16[2,384,768]{2,1,0:T(8,128)(2,1)S(1)} %collective-permute-done.3.refs_6_) | copy-start | bytes 3538948
  21.1 31.4 %collective-permute-start.7 = (bf16[2,384,768]{2,1,0:T(8,128)(2,1)S(1)}, bf16[2,384,768]{2,1,0:T(8,128)(2,1)S(1)}, u32[]{:S(2)}, u32[]{:S(2)}) collective-permute-start(bf16[2,384,768]{2,1,0:T(8,128)(2,1)S(1)} %collective-permute-done.1.refs_8_.refs_9_), channel_id=1, source_target_pairs={{0,192},{1,49},{16,208},{17,1},{32,224},{33,17},{48,240},{49,33},{... | collective-permute-start | bytes 3538952 | tf_op jit(solution)/shard_map/ppermute | solution.py:64
  44.0 41.0 %copy-start.3 = (bf16[2,384,768]{2,1,0:T(8,128)(2,1)}, bf16[2,384,768]{2,1,0:T(8,128)(2,1)S(1)}, u32[]{:S(2)}) copy-start(bf16[2,384,768]{2,1,0:T(8,128)(2,1)S(1)} %collective-permute-done.4.refs_10_.refs_11_) | copy-start | bytes 3538948
  44.0 31.2 %collective-permute-start.12 = (bf16[2,384,768]{2,1,0:T(8,128)(2,1)S(1)}, bf16[2,384,768]{2,1,0:T(8,128)(2,1)S(1)}, u32[]{:S(2)}, u32[]{:S(2)}) collective-permute-start(bf16[2,384,768]{2,1,0:T(8,128)(2,1)S(1)} %collective-permute-done.3.refs_6_), channel_id=1, source_target_pairs={{0,2},{1,15},{2,4},{3,1},{4,6},{5,3},{6,8},{7,5},{8,10},{9,7},{10,... | collective-permute-start | bytes 3538952 | tf_op jit(solution)/shard_map/ppermute | solution.py:63
  49.2 62.8 %copy-start.4 = (bf16[2,384,768]{2,1,0:T(8,128)(2,1)}, bf16[2,384,768]{2,1,0:T(8,128)(2,1)S(1)}, u32[]{:S(2)}) copy-start(bf16[2,384,768]{2,1,0:T(8,128)(2,1)S(1)} %collective-permute-done.11.refs_11_.refs_12_) | copy-start | bytes 3538948
  49.2 28.9 %collective-permute-start.13 = (bf16[2,384,768]{2,1,0:T(8,128)(2,1)S(1)}, bf16[2,384,768]{2,1,0:T(8,128)(2,1)}, u32[]{:S(2)}, u32[]{:S(2)}) collective-permute-start(bf16[2,384,768]{2,1,0:T(8,128)(2,1)S(1)} %collective-permute-done.1.refs_8_.refs_9_), channel_id=1, source_target_pairs={{0,64},{1,17},{16,80},{17,33},{32,96},{33,49},{48,112},{49,1},{64,... | collective-permute-start | bytes 3538952 | tf_op jit(solution)/shard_map/ppermute | solution.py:64
  50.8 61.3 %copy-start.5 = (bf16[2,384,768]{2,1,0:T(8,128)(2,1)}, bf16[2,384,768]{2,1,0:T(8,128)(2,1)S(1)}, u32[]{:S(2)}) copy-start(bf16[2,384,768]{2,1,0:T(8,128)(2,1)S(1)} %collective-permute-done.2.refs_1_) | copy-start | bytes 3538948
  50.8 31.0 %collective-permute-start.10 = (bf16[2,384,768]{2,1,0:T(8,128)(2,1)S(1)}, bf16[2,384,768]{2,1,0:T(8,128)(2,1)}, u32[]{:S(2)}, u32[]{:S(2)}) collective-permute-start(bf16[2,384,768]{2,1,0:T(8,128)(2,1)S(1)} %collective-permute-done.refs_9_.refs_10_), channel_id=1, source_target_pairs={{0,192},{1,49},{16,208},{17,1},{32,224},{33,17},{48,240},{49,33},{... | collective-permute-start | bytes 3538952 | tf_op jit(solution)/shard_map/ppermute | solution.py:64
  52.5 59.7 %copy-start.6 = (bf16[2,384,768]{2,1,0:T(8,128)(2,1)}, bf16[2,384,768]{2,1,0:T(8,128)(2,1)S(1)}, u32[]{:S(2)}) copy-start(bf16[2,384,768]{2,1,0:T(8,128)(2,1)S(1)} %collective-permute-done.5.refs_12_.refs_13_) | copy-start | bytes 3538948
  52.5 29.3 %collective-permute-start.6 = (bf16[2,384,768]{2,1,0:T(8,128)(2,1)S(1)}, bf16[2,384,768]{2,1,0:T(8,128)(2,1)S(1)}, u32[]{:S(2)}, u32[]{:S(2)}) collective-permute-start(bf16[2,384,768]{2,1,0:T(8,128)(2,1)S(1)} %collective-permute-done.2.refs_1_), channel_id=1, source_target_pairs={{0,14},{1,3},{2,0},{3,5},{4,2},{5,7},{6,4},{7,9},{8,6},{9,11},{10,... | collective-permute-start | bytes 3538952 | tf_op jit(solution)/shard_map/ppermute | solution.py:63
  52.5 59.7 %copy-start.7 = (bf16[2,384,768]{2,1,0:T(8,128)(2,1)}, bf16[2,384,768]{2,1,0:T(8,128)(2,1)S(1)}, u32[]{:S(2)}) copy-start(bf16[2,384,768]{2,1,0:T(8,128)(2,1)S(1)} %collective-permute-done.7.refs_13_.refs_14_) | copy-start | bytes 3538948
  52.5 32.5 %collective-permute-start.8 = (bf16[2,384,768]{2,1,0:T(8,128)(2,1)S(1)}, bf16[2,384,768]{2,1,0:T(8,128)(2,1)S(1)}, u32[]{:S(2)}, u32[]{:S(2)}) collective-permute-start(bf16[2,384,768]{2,1,0:T(8,128)(2,1)S(1)} %collective-permute-done.refs_9_.refs_10_), channel_id=1, source_target_pairs={{0,64},{1,17},{16,80},{17,33},{32,96},{33,49},{48,112},{49,1},{64,... | collective-permute-start | bytes 3538952 | tf_op jit(solution)/shard_map/ppermute | solution.py:64
  75.2 37.0 %copy-start.8 = (bf16[2,384,768]{2,1,0:T(8,128)(2,1)}, bf16[2,384,768]{2,1,0:T(8,128)(2,1)S(1)}, u32[]{:S(2)}) copy-start(bf16[2,384,768]{2,1,0:T(8,128)(2,1)S(1)} %collective-permute-done.12.refs_5_) | copy-start | bytes 3538948
  75.2 16.6 %collective-permute-start.17 = (bf16[2,384,768]{2,1,0:T(8,128)(2,1)S(1)}, bf16[2,384,768]{2,1,0:T(8,128)(2,1)S(1)}, u32[]{:S(2)}, u32[]{:S(2)}) collective-permute-start(bf16[2,384,768]{2,1,0:T(8,128)(2,1)S(1)} %collective-permute-done.11.refs_11_.refs_12_), channel_id=1, source_target_pairs={{0,192},{1,49},{16,208},{17,1},{32,224},{33,17},{48,240},{49,33},{... | collective-permute-start | bytes 3538952 | tf_op jit(solution)/shard_map/ppermute | solution.py:64
  78.1 27.5 %collective-permute-start.14 = (bf16[2,384,768]{2,1,0:T(8,128)(2,1)S(1)}, bf16[2,384,768]{2,1,0:T(8,128)(2,1)}, u32[]{:S(2)}, u32[]{:S(2)}) collective-permute-start(bf16[2,384,768]{2,1,0:T(8,128)(2,1)S(1)} %collective-permute-done.12.refs_5_), channel_id=1, source_target_pairs={{0,2},{1,15},{2,4},{3,1},{4,6},{5,3},{6,8},{7,5},{8,10},{9,7},{10,... | collective-permute-start | bytes 3538952 | tf_op jit(solution)/shard_map/ppermute | solution.py:63
  81.8 26.5 %collective-permute-start.15 = (bf16[2,384,768]{2,1,0:T(8,128)(2,1)S(1)}, bf16[2,384,768]{2,1,0:T(8,128)(2,1)}, u32[]{:S(2)}, u32[]{:S(2)}) collective-permute-start(bf16[2,384,768]{2,1,0:T(8,128)(2,1)S(1)} %collective-permute-done.4.refs_10_.refs_11_), channel_id=1, source_target_pairs={{0,64},{1,17},{16,80},{17,33},{32,96},{33,49},{48,112},{49,1},{64,... | collective-permute-start | bytes 3538952 | tf_op jit(solution)/shard_map/ppermute | solution.py:64
  81.8 30.4 %copy-start.9 = (bf16[2,384,768]{2,1,0:T(8,128)(2,1)}, bf16[2,384,768]{2,1,0:T(8,128)(2,1)S(1)}, u32[]{:S(2)}) copy-start(bf16[2,384,768]{2,1,0:T(8,128)(2,1)S(1)} %collective-permute-done.6.refs_2_) | copy-start | bytes 3538948
  81.8 30.3 %collective-permute-start.18 = (bf16[2,384,768]{2,1,0:T(8,128)(2,1)S(1)}, bf16[2,384,768]{2,1,0:T(8,128)(2,1)S(1)}, u32[]{:S(2)}, u32[]{:S(2)}) collective-permute-start(bf16[2,384,768]{2,1,0:T(8,128)(2,1)S(1)} %collective-permute-done.4.refs_10_.refs_11_), channel_id=1, source_target_pairs={{0,192},{1,49},{16,208},{17,1},{32,224},{33,17},{48,240},{49,33},{... | collective-permute-start | bytes 3538952 | tf_op jit(solution)/shard_map/ppermute | solution.py:64
  85.0 27.2 %copy-start.10 = (bf16[2,384,768]{2,1,0:T(8,128)(2,1)}, bf16[2,384,768]{2,1,0:T(8,128)(2,1)S(1)}, u32[]{:S(2)}) copy-start(bf16[2,384,768]{2,1,0:T(8,128)(2,1)S(1)} %collective-permute-done.8.refs_16_.refs_17_) | copy-start | bytes 3538948
  85.0 30.1 %collective-permute-start.9 = (bf16[2,384,768]{2,1,0:T(8,128)(2,1)S(1)}, bf16[2,384,768]{2,1,0:T(8,128)(2,1)}, u32[]{:S(2)}, u32[]{:S(2)}) collective-permute-start(bf16[2,384,768]{2,1,0:T(8,128)(2,1)S(1)} %collective-permute-done.6.refs_2_), channel_id=1, source_target_pairs={{0,14},{1,3},{2,0},{3,5},{4,2},{5,7},{6,4},{7,9},{8,6},{9,11},{10,... | collective-permute-start | bytes 3538952 | tf_op jit(solution)/shard_map/ppermute | solution.py:63
  91.8 20.4 %copy-start.11 = (bf16[2,384,768]{2,1,0:T(8,128)(2,1)}, bf16[2,384,768]{2,1,0:T(8,128)(2,1)S(1)}, u32[]{:S(2)}) copy-start(bf16[2,384,768]{2,1,0:T(8,128)(2,1)S(1)} %collective-permute-done.17.refs_17_.refs_18_) | copy-start | bytes 3538948
  91.8 43.2 %collective-permute-start.19 = (bf16[2,384,768]{2,1,0:T(8,128)(2,1)}, bf16[2,384,768]{2,1,0:T(8,128)(2,1)}, u32[]{:S(2)}, u32[]{:S(2)}) collective-permute-start(bf16[2,384,768]{2,1,0:T(8,128)(2,1)} %collective-permute-done.13.refs_14_.refs_15_), channel_id=1, source_target_pairs={{0,64},{1,17},{16,80},{17,33},{32,96},{33,49},{48,112},{49,1},{64,... | collective-permute-start | bytes 3538952 | tf_op jit(solution)/shard_map/ppermute | solution.py:64
  105.6 29.4 %collective-permute-start.20 = (bf16[2,384,768]{2,1,0:T(8,128)(2,1)}, bf16[2,384,768]{2,1,0:T(8,128)(2,1)}, u32[]{:S(2)}, u32[]{:S(2)}) collective-permute-start(bf16[2,384,768]{2,1,0:T(8,128)(2,1)} %collective-permute-done.10.refs_15_.refs_16_), channel_id=1, source_target_pairs={{0,192},{1,49},{16,208},{17,1},{32,224},{33,17},{48,240},{49,33},{... | collective-permute-start | bytes 3538952 | tf_op jit(solution)/shard_map/ppermute | solution.py:64
  108.2 26.7 %collective-permute-start.16 = (bf16[2,384,768]{2,1,0:T(8,128)(2,1)}, bf16[2,384,768]{2,1,0:T(8,128)(2,1)}, u32[]{:S(2)}, u32[]{:S(2)}) collective-permute-start(bf16[2,384,768]{2,1,0:T(8,128)(2,1)} %collective-permute-done.14.refs_4_), channel_id=1, source_target_pairs={{0,2},{1,15},{2,4},{3,1},{4,6},{5,3},{6,8},{7,5},{8,10},{9,7},{10,... | collective-permute-start | bytes 3538952 | tf_op jit(solution)/shard_map/ppermute | solution.py:63
  112.0 1.1 copy-start.12
  112.0 22.9 %collective-permute-start.21 = (bf16[2,384,768]{2,1,0:T(8,128)(2,1)}, bf16[2,384,768]{2,1,0:T(8,128)(2,1)}, u32[]{:S(2)}, u32[]{:S(2)}) collective-permute-start(bf16[2,384,768]{2,1,0:T(8,128)(2,1)} %collective-permute-done.15.refs_18_.refs_19_), channel_id=1, source_target_pairs={{0,64},{1,17},{16,80},{17,33},{32,96},{33,49},{48,112},{49,1},{64,... | collective-permute-start | bytes 3538952 | tf_op jit(solution)/shard_map/ppermute | solution.py:64
